TPU v7x, 32 devices: a whole 2x2x4 slice. The times are simulated.
32 devices in a mesh: groups: 2 (over y), ctx: 4 (over z), exp: 2 (over x), tp: 2 (over core).
Axes of the slice: x: 2, y: 2, z: 4, core: 2. Of those that a mesh axis runs over, the one named last changes fastest.
Arguments:
- query_rows: bfloat16 [1024, 3072], P(('groups', 'ctx'), ('exp', 'tp')), parts along dimension 0, may hold values from -8 to 8
- key_rows: bfloat16 [1024, 512], P(('groups', 'ctx'), 'exp'), parts along dimension 0, may hold values from -8 to 8
- value_rows: bfloat16 [1024, 512], P(('groups', 'ctx'), 'exp'), parts along dimension 0, may hold values from -6 to 6
- residual: bfloat16 [1024, 3072], P(('groups', 'ctx'), ('exp', 'tp')), parts along dimension 0, may hold values from -4 to 4
- norm_gain: float32 [3072], P(('exp', 'tp')), may hold values from 0.5 to 1.5
- router_weight: float32 [3072, 8], P(('exp', 'tp')), may hold values from -0.109375 to 0.109375
- expert_ids: int32 [1024, 2], P(('groups', 'ctx')), parts along dimension 0, may hold values from 0 to 7, all different within a row; in each aligned block of 128 rows (0 to 127, 128 to 255, ...) at most 48 rows name the same one
- gate_weight: bfloat16 [3072, 2, 32768], P('exp', 'tp', 'ctx'), may hold values from -0.109375 to 0.109375
- down_weight: bfloat16 [2, 32768, 3072], P('tp', 'ctx', 'exp'), may hold values from -0.0625 to 0.0625
Outputs:
- layer_out: bfloat16 [1024, 3072], P(('groups', 'ctx'), ('exp', 'tp')), parts along dimension 0
There are 2 independent parts, one for each index of `groups`. A program takes and returns all parts, laid end to end along the dimension named above; an argument that names none is the same for every part. Nothing has to cross between parts.
Inputs may be any that keep to these rules, and one draw needn't show every extreme that they name: `expert_ids`: each token names two different experts; among the 128 tokens of each aligned block no expert is named more than 48 times.
All inputs are finite; a program needn't handle non-finite values.
Results may differ from a plain program's by a relative error of at most 0.012.
Values may be sent and summed in bfloat16 or wider, within the bound.
A program may use at most 192 MiB of HBM per device.

v0:
```python
import math

import jax
import jax.numpy as jnp
from jax import lax
from jax.sharding import PartitionSpec as P

HD = 128
QH = 24
KVH = 4
E = 8
C = 48


epsilon = 1e-05
highest = lax.Precision.HIGHEST
floor_score = -1e30


def per_device(
    query_rows,
    key_rows,
    value_rows,
    residual,
    norm_gain,
    router_weight,
    expert_ids,
    gate_weight,
    down_weight,
):
    ctx_count = lax.axis_size("ctx")
    row_count = query_rows.shape[0]
    kv_local = key_rows.shape[1] // HD
    query_local = query_rows.shape[1] // HD
    group_size = QH // KVH
    first_row = lax.axis_index("ctx") * row_count
    query_pos = first_row + jnp.arange(row_count, dtype=jnp.int32)
    query_heads = query_rows.reshape(row_count, query_local, HD)
    head_owner = (
        lax.axis_index("tp") * query_local + jnp.arange(query_local, dtype=jnp.int32)
    ) // group_size
    head_select = (head_owner[:, None] == jnp.arange(kv_local, dtype=jnp.int32)[None, :]).astype(
        jnp.bfloat16
    )
    score_scale = 1.0 / math.sqrt(HD)
    key_piece = lax.all_gather(key_rows, "ctx", axis=0, tiled=True)
    value_piece = lax.all_gather(value_rows, "ctx", axis=0, tiled=True)
    width_keys = key_piece.shape[0]
    key_heads = jnp.einsum(
        "shd,qh->sqd",
        key_piece.reshape(width_keys, kv_local, HD),
        head_select,
        preferred_element_type=jnp.float32,
    ).astype(jnp.bfloat16)
    value_heads = jnp.einsum(
        "shd,qh->sqd",
        value_piece.reshape(width_keys, kv_local, HD),
        head_select,
        preferred_element_type=jnp.float32,
    )
    key_pos = jnp.arange(width_keys, dtype=jnp.int32)
    visible = query_pos[:, None] >= key_pos[None, :]
    run_max = jnp.full((query_local, row_count), floor_score, jnp.float32)
    scores = (
        jnp.einsum("tqd,sqd->qts", query_heads, key_heads, preferred_element_type=jnp.float32)
        * score_scale
    )
    scores = jnp.where(visible, scores, floor_score)
    new_max = jnp.maximum(run_max, jnp.max(scores, axis=-1))
    weights = jnp.where(visible, jnp.exp(scores - new_max[..., None]), 0.0)
    run_total = jnp.sum(weights, axis=-1)
    accumulated = jnp.einsum("qts,sqd->qtd", weights, value_heads, precision=highest)
    run_max, run_total, accumulated = (new_max, run_total, accumulated)
    attended = jnp.transpose(accumulated / run_total[..., None], (1, 0, 2)).reshape(row_count, -1)
    mixed_in = residual.astype(jnp.float32) + attended
    scaled = mixed_in * norm_gain[None, :]
    square_sum, logit_part = lax.psum(
        (jnp.sum(mixed_in * mixed_in, axis=1), jnp.dot(scaled, router_weight, precision=highest)),
        ("exp", "tp"),
    )
    inv_rms = lax.rsqrt(square_sum / (QH * HD) + epsilon)
    moe_half = (scaled * inv_rms[:, None]).astype(jnp.bfloat16)
    logits = logit_part * inv_rms[:, None]
    expert_range = jnp.arange(E, dtype=jnp.int32)
    chosen_hot = expert_ids[:, :, None] == expert_range[None, None, :]
    picked = jnp.sum(jnp.where(chosen_hot, logits[:, None, :], 0.0), axis=2)
    gate_pair = jnp.stack(
        [jax.nn.sigmoid(picked[:, 0] - picked[:, 1]), jax.nn.sigmoid(picked[:, 1] - picked[:, 0])],
        axis=1,
    )
    flat_ids = expert_ids.reshape(-1)
    flat_hot = (flat_ids[:, None] == expert_range[None, :]).astype(jnp.int32)
    slot_index = jnp.sum((jnp.cumsum(flat_hot, axis=0) - flat_hot) * flat_hot, axis=1)
    tile_row = (flat_ids * C + slot_index).reshape(row_count, 2)
    tile_range = jnp.arange(E * C, dtype=jnp.int32)
    tile_hot = tile_row[:, :, None] == tile_range[None, None, :]
    combine_matrix = jnp.sum(jnp.where(tile_hot, gate_pair[:, :, None], 0.0), axis=1)
    dispatch_matrix = jnp.transpose(jnp.any(tile_hot, axis=1)).astype(jnp.bfloat16)
    ctx_sharing = max(1, ctx_count // E)
    experts_held = max(1, E // ctx_count)
    feature_rows = lax.all_gather(moe_half, "tp", axis=1, tiled=True)
    feature_width = feature_rows.shape[1]
    send_tiles = jnp.dot(dispatch_matrix, feature_rows, preferred_element_type=jnp.float32).astype(
        jnp.bfloat16
    )
    send_tiles = send_tiles.reshape(E, C, feature_width)
    outgoing = jnp.repeat(send_tiles, ctx_sharing, axis=0).reshape(
        ctx_count, experts_held, C, feature_width
    )
    arrived = lax.all_to_all(outgoing, "ctx", split_axis=0, concat_axis=0, tiled=True)
    local_gate = gate_weight.reshape(gate_weight.shape[0], experts_held, -1)
    local_down = down_weight.reshape(experts_held, -1, down_weight.shape[2])
    partial_pre = jnp.einsum(
        "secd,deh->sech", arrived, local_gate, preferred_element_type=jnp.float32
    )
    total_pre = lax.psum(partial_pre.astype(jnp.bfloat16), "exp").astype(jnp.float32)
    hidden = jax.nn.silu(total_pre).astype(jnp.bfloat16)
    expert_part = jnp.einsum(
        "sech,ehd->secd", hidden, local_down, preferred_element_type=jnp.float32
    )
    core_summed = lax.psum_scatter(
        expert_part.astype(jnp.bfloat16), "tp", scatter_dimension=3, tiled=True
    ).astype(jnp.float32)
    returned = lax.all_to_all(
        core_summed.astype(jnp.bfloat16), "ctx", split_axis=0, concat_axis=0, tiled=True
    ).astype(core_summed.dtype)
    width_out = returned.shape[3]
    summed = jnp.sum(returned.reshape(E, ctx_sharing, C, width_out), axis=1).reshape(
        E * C, width_out
    )
    moe_mine = jnp.dot(combine_matrix, summed, precision=highest)
    return (mixed_in + moe_mine).astype(jnp.bfloat16)


def solution(mesh):
    return jax.shard_map(
        per_device,
        mesh=mesh,
        in_specs=(
            P(("groups", "ctx"), ("exp", "tp")),
            P(("groups", "ctx"), "exp"),
            P(("groups", "ctx"), "exp"),
            P(("groups", "ctx"), ("exp", "tp")),
            P(("exp", "tp")),
            P(("exp", "tp"), None),
            P(("groups", "ctx"), None),
            P("exp", "tp", "ctx"),
            P("tp", "ctx", "exp"),
        ),
        out_specs=P(("groups", "ctx"), ("exp", "tp")),
        check_vma=False,
    )
```

profile of v0, /device:TPU:0, one launch (start us, length us, event | category | flops | bytes accessed | tf_op | source)
XLA Modules:
  0.0 272.8 jit_solution(11050796885780323103)
XLA Ops:
  6.5 0.0 copy-start
  6.5 0.8 copy.67
  7.3 0.1 eq.71
  7.5 0.1 eq.67
  7.7 15.8 %all_gather.9 = bf16[512,256]{1,0:T(8,128)(2,1)S(1)} all-gather(bf16[128,256]{1,0:T(8,128)(2,1)} %param.10), channel_id=1, replica_groups=mesh['groups'=2,'ctx'=4,'exp'=2,'tp'=2] {'ctx'}, dimensions={0}, use_global_device_ids=true | all-gather | bytes 327680 | tf_op jit(solution)/shard_map/all_gather | solution.py:46
  23.5 0.1 reshape.74
  23.6 1.1 copy.61
  24.7 0.0 copy-start.3
  24.7 0.5 fusion.23
  25.2 0.4 fusion.50
  25.7 14.4 %all_gather.10 = bf16[512,256]{1,0:T(8,128)(2,1)S(1)} all-gather(bf16[128,256]{1,0:T(8,128)(2,1)S(1)} %copy-done.3), channel_id=1, replica_groups=mesh['groups'=2,'ctx'=4,'exp'=2,'tp'=2] {'ctx'}, dimensions={0}, use_global_device_ids=true | all-gather | bytes 327680 | tf_op jit(solution)/shard_map/all_gather | solution.py:47
  40.1 0.1 reshape.76
  40.2 0.5 convolution_bitcast_fusion
  40.7 0.3 fusion.24
  41.0 0.0 copy-start.2
  41.0 0.0 copy-start.4
  41.0 3.1 %fusion.28 = f32[128,6,128]{0,2,1:T(8,128)S(1)} fusion(f32[512,6,128]{2,1,0:T(8,128)S(1)} %convolution_bitcast_fusion, f32[6,128,512]{1,2,0:T(8,128)S(1)} %get-tuple-element.10, f32[6,128]{1,0:T(8,128)S(1)} %broadcast_maximum_fusion, pred[128,512]{0,1:T(8,128)(4,1)S(1)} %iota_compare_fusion.1, f32[128,6]{0,1:T(8,128)S(1)} %bitcast.53), kind=kOutput, calls=%fused_computation.24 | convolution fusion | flops 604864512 | bytes 3610624 | tf_op jit(solution)/shard_map/qts,sqd->qtd/dot_general | solution.py:72
  44.1 0.0 copy-start.5
  44.1 0.2 copy.66
  44.3 0.1 multiply_reduce_fusion
  44.4 0.0 copy-done.4
  44.4 0.4 fusion.38
  44.9 5.8 %all-reduce = (f32[128,8]{0,1:T(8,128)S(1)}, f32[128]{0:T(128)S(1)}) all-reduce(f32[128,8]{0,1:T(8,128)S(1)} %fusion.38, f32[128]{0:T(128)S(1)} %multiply_reduce_fusion), channel_id=1, replica_groups=mesh['groups'=2,'ctx'=4,'exp'=2,'tp'=2] {'exp','tp'}, use_global_device_ids=true, to_apply=%region_5.6 | all-reduce | flops 1152 | bytes 9216 | tf_op jit(solution)/shard_map/psum | solution.py:77
  50.6 0.1 multiply_convert_fusion
  50.7 2.1 all_gather.11
  52.8 0.6 reduce-window.6
  53.4 0.2 slice_reduce_fusion
  53.6 0.1 fusion.42
  53.7 0.1 reduce_sum.53
  53.9 0.1 copy.69
  54.0 0.1 fusion.37
  54.1 1.6 convolution_convert_fusion
  55.7 4.6 %all-to-all-start = ((bf16[4,2,48,1536]{3,2,1,0:T(8,128)(2,1)}), bf16[4,2,48,1536]{3,2,1,0:T(8,128)(2,1)S(1)}, u32[]{:S(2)}, u32[]{:S(2)}) async-start(bf16[4,2,48,1536]{3,2,1,0:T(8,128)(2,1)} %bitcast.10), calls=%async_computation | async-start | bytes 2359296 | tf_op jit(solution)/shard_map/all_to_all | solution.py:110
  60.4 41.0 %reshape.79 = bf16[1536,2,4096]{2,1,0:T(2,128)(2,1)} reshape(bf16[1536,1,8192]{2,0,1:T(8,128)(2,1)} %param.16) | data formatting | bytes 50331648 | tf_op jit(solution)/shard_map/reshape | solution.py:111
  101.4 0.0 all-to-all-done
  101.4 31.1 %fusion.9 = bf16[4,2,48,4096]{3,2,0,1:T(8,128)(2,1)} fusion(bf16[1536,2,4096,1]{2,1,0,3:T(2,128)(2,1)} %bitcast.49, bf16[4,2,48,1536]{3,2,1,0:T(8,128)(2,1)S(1)} %all-to-all-done), kind=kOutput, calls=%fused_computation.9 | convolution fusion | flops 4833411072 | bytes 29491200 | tf_op jit(solution)/shard_map/secd,deh->sech/dot_general | solution.py:113
  132.5 0.0 all-reduce.3.cloned.1.call-update
  132.5 0.0 reduce-scatter.2.cloned.1.call-start
  132.6 87.6 %all-reduce.3.cloned.1.call-done = bf16[4,2,48,4096]{3,2,0,1:T(8,128)(2,1)} async-done(((bf16[4,2,48,4096]{3,2,0,1:T(8,128)(2,1)}), bf16[4,2,48,4096]{3,2,0,1:T(8,128)(2,1)}) %all-reduce.3.cloned.1.call-update) | async-done | bytes 3145744 | tf_op jit(solution)/shard_map/psum | solution.py:116
  220.2 12.6 %fusion.18 = bf16[4,2,48,1536]{3,2,0,1:T(8,128)(2,1)} fusion(bf16[2,4096,1536,1]{2,1,3,0:T(8,128)(2,1)} %bitcast.54, bf16[4,2,48,4096]{3,2,0,1:T(8,128)(2,1)} %all-reduce.3.cloned.1.call-done), kind=kOutput, calls=%fused_computation.14 | convolution fusion | flops 4841865216 | bytes 29491200 | tf_op jit(solution)/shard_map/sech,ehd->secd/dot_general | solution.py:118
  232.8 0.0 reduce-scatter.2.cloned.1.call-update
  232.8 0.0 copy-start.1
  232.8 8.8 %reduce-scatter.2.cloned.1.call-done = bf16[4,2,48,768]{3,2,0,1:T(8,128)(2,1)} async-done(((bf16[4,2,48,1536]{3,2,0,1:T(8,128)(2,1)}), bf16[4,2,48,768]{3,2,0,1:T(8,128)(2,1)}) %reduce-scatter.2.cloned.1.call-update) | async-done | bytes 589840 | tf_op jit(solution)/shard_map/reduce_scatter | solution.py:121
  241.6 1.9 copy.72
  243.5 4.9 %all-to-all-start.1 = ((bf16[4,2,48,768]{3,2,1,0:T(8,128)(2,1)}), bf16[4,2,48,768]{3,2,1,0:T(8,128)(2,1)S(1)}, u32[]{:S(2)}, u32[]{:S(2)}) async-start(bf16[4,2,48,768]{3,2,1,0:T(8,128)(2,1)} %copy.72), calls=%async_computation.2 | async-start | bytes 1179648 | tf_op jit(solution)/shard_map/all_to_all | solution.py:124
  248.5 0.1 select_reduce_fusion
  248.6 16.1 %all-to-all-done.1 = bf16[4,2,48,768]{3,2,1,0:T(8,128)(2,1)S(1)} async-done(((bf16[4,2,48,768]{3,2,1,0:T(8,128)(2,1)}), bf16[4,2,48,768]{3,2,1,0:T(8,128)(2,1)S(1)}, u32[]{:S(2)}, u32[]{:S(2)}) %all-to-all-start.1) | async-done | bytes 589856 | tf_op jit(solution)/shard_map/all_to_all | solution.py:124
  264.8 1.2 fusion.32
  (19 shorter events, 0.2 us)
Async XLA Ops:
  6.5 37.9 %copy-start = (f32[768,8]{0,1:T(8,128)S(1)}, f32[768,8]{0,1:T(8,128)}, u32[]{:S(2)}) copy-start(f32[768,8]{0,1:T(8,128)} %param.14) | copy-start | bytes 73732
  24.7 1.0 copy-start.3
  41.0 3.3 %copy-start.2 = (bf16[128,768]{1,0:T(8,128)(2,1)S(1)}, bf16[128,768]{1,0:T(8,128)(2,1)}, u32[]{:S(2)}) copy-start(bf16[128,768]{1,0:T(8,128)(2,1)} %param.12) | copy-start | bytes 589828
  41.0 3.4 %copy-start.4 = (f32[768]{0:T(1024)S(1)}, f32[768]{0:T(1024)}, u32[]{:S(2)}) copy-start(f32[768]{0:T(1024)} %param.13) | copy-start | bytes 9220
  44.1 9.9 %copy-start.5 = (s32[128,2]{0,1:T(2,128)S(1)}, s32[128,2]{0,1:T(2,128)}, u32[]{:S(2)}) copy-start(s32[128,2]{0,1:T(2,128)} %param.15) | copy-start | bytes 3076
  55.7 45.6 %all-to-all-start = ((bf16[4,2,48,1536]{3,2,1,0:T(8,128)(2,1)}), bf16[4,2,48,1536]{3,2,1,0:T(8,128)(2,1)S(1)}, u32[]{:S(2)}, u32[]{:S(2)}) async-start(bf16[4,2,48,1536]{3,2,1,0:T(8,128)(2,1)} %bitcast.10), calls=%async_computation | async-start | bytes 2359296 | tf_op jit(solution)/shard_map/all_to_all | solution.py:110
  60.4 159.8 %all-reduce.3.cloned.1.call-start = ((), (), s32[]{:S(2)}) async-start(), calls=%async_computation.3 | async-start | bytes 6291456 | tf_op jit(solution)/shard_map/psum | solution.py:116
  132.5 109.1 %reduce-scatter.2.cloned.1.call-start = ((), (), s32[]{:S(2)}) async-start(), calls=%async_computation.4 | async-start | bytes 1769472 | tf_op jit(solution)/shard_map/reduce_scatter | solution.py:121
  232.8 33.1 %copy-start.1 = (f32[768,8]{0,1:T(8,128)S(1)}, f32[768,8]{0,1:T(8,128)}, u32[]{:S(2)}) copy-start(f32[768,8]{0,1:T(8,128)} %param.14) | copy-start | bytes 73732
  243.5 21.2 %all-to-all-start.1 = ((bf16[4,2,48,768]{3,2,1,0:T(8,128)(2,1)}), bf16[4,2,48,768]{3,2,1,0:T(8,128)(2,1)S(1)}, u32[]{:S(2)}, u32[]{:S(2)}) async-start(bf16[4,2,48,768]{3,2,1,0:T(8,128)(2,1)} %copy.72), calls=%async_computation.2 | async-start | bytes 1179648 | tf_op jit(solution)/shard_map/all_to_all | solution.py:124
Sparse Core Ops, SparseCore 0:
  132.6 87.4 all-reduce.2
  232.9 8.6 reduce-scatter.1
where the time goes:
time: 274 us; the launch traced here: 273 us
  waiting for transfers between devices  113 us (41%)
  matrix products  51.4 us (19%)
  local copies, waits for them, and re-layouts  45.8 us (17%)
  blocking collectives  38.1 us (14%)
  between operations  13.6 us (5%)
  starting transfers between devices  9.55 us (3%)
    psum x1, waiting for transfers between devices, per_device(): lax.psum(partial_pre.astype(jnp.bfloat16), 'exp').astype(jnp.float32)  87.6 us
    reshape x1, local copies, waits for them, and re-layouts, per_device(): local_gate = gate_weight.reshape(gate_weight.shape[0], experts_held, -1)  41 us
    dot_general x1, matrix products, per_device(): jnp.einsum('secd,deh->sech', arrived, local_gate, preferred_element_type=...  31.1 us
    all_to_all x1, waiting for transfers between devices, per_device(): lax.all_to_all(core_summed.astype(jnp.bfloat16), 'ctx', split_axis=0, con...  16.1 us
    all_gather x1, blocking collectives, per_device(): key_piece = lax.all_gather(key_rows, 'ctx', axis=0, tiled=True)  15.8 us
    all_gather x1, blocking collectives, per_device(): value_piece = lax.all_gather(value_rows, 'ctx', axis=0, tiled=True)  14.4 us
    dot_general x1, matrix products, per_device(): jnp.einsum('sech,ehd->secd', hidden, local_down, preferred_element_type=j...  12.6 us
    reduce_scatter x1, waiting for transfers between devices, per_device(): lax.psum_scatter(expert_part.astype(jnp.bfloat16), 'tp', scatter_dimensio...  8.81 us
  transfers between devices with their start and end apart: 4, of which 3 were waited for; matrix products, arithmetic and copies ran while one was open for 15% of the time, Pallas kernels for 0%

commit v1 on v0

v1 whole, which is shorter than its diff:
```python
import math

import jax
import jax.numpy as jnp
from jax import lax
from jax.sharding import PartitionSpec as P

HD = 128
QH = 24
KVH = 4
E = 8
C = 48
PIECES = 2


epsilon = 1e-05
highest = lax.Precision.HIGHEST
floor_score = -1e30


def per_device(
    query_rows,
    key_rows,
    value_rows,
    residual,
    norm_gain,
    router_weight,
    expert_ids,
    gate_weight,
    down_weight,
):
    ctx_count = lax.axis_size("ctx")
    exp_count = lax.axis_size("exp")
    tp_count = lax.axis_size("tp")
    tp_index = lax.axis_index("tp")
    row_count = query_rows.shape[0]
    kv_local = key_rows.shape[1] // HD
    query_local = query_rows.shape[1] // HD
    group_size = QH // KVH
    assert group_size % query_local == 0 and tp_count == 2
    owner = (tp_index * query_local) // group_size
    first_row = lax.axis_index("ctx") * row_count
    query_pos = first_row + jnp.arange(row_count, dtype=jnp.int32)
    query_heads = query_rows.reshape(row_count, query_local, HD)

    def own_head(rows):
        return lax.dynamic_slice_in_dim(rows, owner * HD, HD, axis=1)

    pair = jnp.concatenate([own_head(key_rows), own_head(value_rows)], axis=1)
    pair = lax.all_gather(pair, "ctx", axis=0, tiled=True)
    key_head, value_head = pair[:, :HD], pair[:, HD:]
    visible = query_pos[:, None] >= jnp.arange(pair.shape[0], dtype=jnp.int32)[None, :]
    scores = jnp.einsum(
        "tqd,sd->qts", query_heads, key_head, preferred_element_type=jnp.float32
    ) * (1.0 / math.sqrt(HD))
    scores = jnp.where(visible[None], scores, floor_score)
    weights = jnp.exp(scores - jnp.max(scores, axis=-1, keepdims=True))
    run_total = jnp.sum(weights, axis=-1, keepdims=True)
    accumulated = jnp.einsum(
        "qts,sd->qtd",
        weights.astype(jnp.bfloat16),
        value_head,
        preferred_element_type=jnp.float32,
    )
    attended = jnp.transpose(accumulated / run_total, (1, 0, 2)).reshape(row_count, -1)
    mixed_in = residual.astype(jnp.float32) + attended
    scaled = mixed_in * norm_gain[None, :]
    square_sum, logit_part = lax.psum(
        (jnp.sum(mixed_in * mixed_in, axis=1), jnp.dot(scaled, router_weight, precision=highest)),
        ("exp", "tp"),
    )
    inv_rms = lax.rsqrt(square_sum / (QH * HD) + epsilon)
    moe_half = (scaled * inv_rms[:, None]).astype(jnp.bfloat16)
    logits = logit_part * inv_rms[:, None]
    expert_range = jnp.arange(E, dtype=jnp.int32)
    chosen_hot = expert_ids[:, :, None] == expert_range[None, None, :]
    picked = jnp.sum(jnp.where(chosen_hot, logits[:, None, :], 0.0), axis=2)
    gate_pair = jnp.stack(
        [jax.nn.sigmoid(picked[:, 0] - picked[:, 1]), jax.nn.sigmoid(picked[:, 1] - picked[:, 0])],
        axis=1,
    )
    flat_ids = expert_ids.reshape(-1)
    flat_hot = (flat_ids[:, None] == expert_range[None, :]).astype(jnp.int32)
    slot_index = jnp.sum((jnp.cumsum(flat_hot, axis=0) - flat_hot) * flat_hot, axis=1)
    tile_row = (flat_ids * C + slot_index).reshape(row_count, 2)
    tile_range = jnp.arange(E * C, dtype=jnp.int32)
    tile_hot = tile_row[:, :, None] == tile_range[None, None, :]
    combine_matrix = jnp.sum(jnp.where(tile_hot, gate_pair[:, :, None], 0.0), axis=1)
    dispatch_matrix = jnp.transpose(jnp.any(tile_hot, axis=1)).astype(jnp.bfloat16)
    ctx_sharing = max(1, ctx_count // E)
    experts_held = max(1, E // ctx_count)
    send_tiles = jnp.dot(dispatch_matrix, moe_half, preferred_element_type=jnp.float32).astype(
        jnp.bfloat16
    )
    send_tiles = send_tiles.reshape(E, C, -1)
    outgoing = jnp.repeat(send_tiles, ctx_sharing, axis=0).reshape(ctx_count, experts_held, C, -1)
    hidden_width = gate_weight.shape[2] // experts_held
    pieces = max(1, min(PIECES, hidden_width // 512))
    piece = hidden_width // pieces
    arrived = []
    for e in range(experts_held):
        half = lax.all_to_all(outgoing[:, e], "ctx", split_axis=0, concat_axis=0, tiled=True)
        arrived.append(
            lax.all_gather(half.reshape(ctx_count * C, -1), "tp", axis=1, tiled=True)
        )
    sums = []
    for e in range(experts_held):
        for i in range(pieces):
            low = e * hidden_width + i * piece
            part = jnp.dot(
                arrived[e],
                gate_weight[:, 0, low : low + piece],
                preferred_element_type=jnp.float32,
            ).astype(jnp.bfloat16)
            total = part.astype(jnp.float32)
            for shift in range(1, exp_count):
                turned = [(j, (j + shift) % exp_count) for j in range(exp_count)]
                total = total + lax.ppermute(part, "exp", turned).astype(jnp.float32)
            sums.append(total)
    width_out = down_weight.shape[2] // tp_count
    moe_mine = 0.0
    combine_parts = combine_matrix.reshape(row_count, -1, experts_held, C)
    for e in range(experts_held):
        out = 0.0
        for i in range(pieces):
            low = e * hidden_width + i * piece
            hidden = jax.nn.silu(sums[e * pieces + i]).astype(jnp.bfloat16)
            out = out + jnp.dot(
                hidden, down_weight[0, low : low + piece], preferred_element_type=jnp.float32
            )
        low_half, high_half = out[:, :width_out], out[:, width_out:]
        mine = jnp.where(tp_index == 0, low_half, high_half)
        other = jnp.where(tp_index == 0, high_half, low_half).astype(jnp.bfloat16)
        swapped = lax.ppermute(other, "tp", [(0, 1), (1, 0)])
        core_summed = (mine + swapped.astype(jnp.float32)).astype(jnp.bfloat16)
        returned = lax.all_to_all(
            core_summed.reshape(ctx_count, C, width_out),
            "ctx",
            split_axis=0,
            concat_axis=0,
            tiled=True,
        ).astype(jnp.float32)
        summed = jnp.sum(returned.reshape(-1, ctx_sharing, C, width_out), axis=1)
        moe_mine = moe_mine + jnp.dot(
            combine_parts[:, :, e].reshape(row_count, -1),
            summed.reshape(-1, width_out),
            precision=highest,
        )
    return (mixed_in + moe_mine).astype(jnp.bfloat16)


def solution(mesh):
    return jax.shard_map(
        per_device,
        mesh=mesh,
        in_specs=(
            P(("groups", "ctx"), ("exp", "tp")),
            P(("groups", "ctx"), "exp"),
            P(("groups", "ctx"), "exp"),
            P(("groups", "ctx"), ("exp", "tp")),
            P(("exp", "tp")),
            P(("exp", "tp"), None),
            P(("groups", "ctx"), None),
            P("exp", "tp", "ctx"),
            P("tp", "ctx", "exp"),
        ),
        out_specs=P(("groups", "ctx"), ("exp", "tp")),
        check_vma=False,
    )
```

time: 274 us -> 163 us (0.59)
  local copies, waits for them, and re-layouts: 45.8 us -> 4.9 us
  waiting for transfers between devices: 113 us -> 74 us
  matrix products: 51.4 us -> 31.6 us
  between operations: 13.6 us -> 0.4 us
  blocking collectives: 38.1 us -> 26 us
  starting transfers between devices: 9.55 us -> 21.6 us
    psum x1 -> x0, waiting for transfers between devices: 87.6 us -> none  [per_device(): lax.psum(partial_pre.astype(jnp.bfloat16), 'exp').astype(jnp.float32)]
    ppermute x0 -> x6, waiting for transfers between devices: none -> 47.1 us  [the longest x4 47.1 us: per_device(): total = total + lax.ppermute(part, 'exp', turned).astype(jnp.float32)]
    reshape x4 -> x1, local copies, waits for them, and re-layouts: 41.3 us -> 0.16 us  [per_device(): jnp.transpose(accumulated / run_total, (1, 0, 2)).reshape(row_count, -1)]
    dot_general x8 -> x13, matrix products: 51 us -> 31.2 us  [the longest x4 17.3 us: per_device(): jnp.dot(arrived[e], gate_weight[:, 0, low:low + piece], preferred_element...]
    all_gather x3, blocking collectives: 32.4 us -> 20.3 us  [the longest x1 15.6 us: per_device(): pair = lax.all_gather(pair, 'ctx', axis=0, tiled=True)]
    all_to_all x2 -> x4, waiting for transfers between devices: 16.1 us -> 26.9 us  [the longest x2 17.3 us: per_device(): lax.all_to_all(core_summed.reshape(ctx_count, C, width_out), 'ctx', split...]
    reduce_scatter x1 -> x0, waiting for transfers between devices: 8.81 us -> none  [per_device(): lax.psum_scatter(expert_part.astype(jnp.bfloat16), 'tp', scatter_dimensio...]
    all_to_all x2 -> x4, starting transfers between devices: 9.5 us -> 17.2 us  [the longest x2 8.62 us: per_device(): lax.all_to_all(core_summed.reshape(ctx_count, C, width_out), 'ctx', split...]
  transfers between devices with their start and end apart: 4 -> 10, of which waited for: 3 -> 7; matrix products, arithmetic and copies ran while one was open for 15% -> 19% of each run, Pallas kernels for 0% -> 0%
where the time goes in v1:
time: 163 us; the launch traced here: 162 us
  waiting for transfers between devices  74 us (45%)
  matrix products  31.6 us (19%)
  blocking collectives  26 us (16%)
  starting transfers between devices  21.6 us (13%)
  local copies, waits for them, and re-layouts  4.9 us (3%)
  other arithmetic  3.17 us (2%)
    ppermute x4, waiting for transfers between devices, per_device(): total = total + lax.ppermute(part, 'exp', turned).astype(jnp.float32)  47.1 us
    all_to_all x2, waiting for transfers between devices, per_device(): lax.all_to_all(core_summed.reshape(ctx_count, C, width_out), 'ctx', split...  17.3 us
    dot_general x4, matrix products, per_device(): jnp.dot(arrived[e], gate_weight[:, 0, low:low + piece], preferred_element...  17.3 us
    all_gather x1, blocking collectives, per_device(): pair = lax.all_gather(pair, 'ctx', axis=0, tiled=True)  15.6 us
    dot_general x4, matrix products, per_device(): jnp.dot(hidden, down_weight[0, low:low + piece], preferred_element_type=j...  11.3 us
    all_to_all x2, waiting for transfers between devices, per_device(): lax.all_to_all(outgoing[:, e], 'ctx', split_axis=0, concat_axis=0, tiled=...  9.6 us
    all_to_all x2, starting transfers between devices, per_device(): lax.all_to_all(core_summed.reshape(ctx_count, C, width_out), 'ctx', split...  8.62 us
    all_to_all x2, starting transfers between devices, per_device(): lax.all_to_all(outgoing[:, e], 'ctx', split_axis=0, concat_axis=0, tiled=...  8.62 us
  transfers between devices with their start and end apart: 10, of which 7 were waited for; matrix products, arithmetic and copies ran while one was open for 19% of the time, Pallas kernels for 0%

profile of v1, /device:TPU:0, one launch (start us, length us, event | category | flops | bytes accessed | tf_op | source)
XLA Modules:
  0.0 161.7 jit_solution(9638693283296045638)
XLA Ops:
  0.0 0.8 copy.56
  0.8 0.1 eq.61
  0.9 0.1 eq.57
  1.1 0.8 constant_dynamic-slice_fusion
  1.9 15.6 %all_gather.9 = bf16[512,256]{1,0:T(8,128)(2,1)S(1)} all-gather(bf16[128,256]{1,0:T(8,128)(2,1)S(1)} %pad_maximum_fusion), channel_id=1, replica_groups=mesh['groups'=2,'ctx'=4,'exp'=2,'tp'=2] {'ctx'}, dimensions={0}, use_global_device_ids=true | all-gather | bytes 327680 | tf_op jit(solution)/shard_map/all_gather | solution.py:50
  17.6 1.1 copy.51
  18.7 0.4 fusion.67
  19.1 0.2 fusion.42
  19.3 0.4 fusion.44
  19.7 0.2 copy.55
  19.9 0.3 copy-done.2
  20.4 0.4 fusion.54
  20.8 5.8 %all-reduce = (f32[128,8]{0,1:T(8,128)S(1)}, f32[128]{0:T(128)S(1)}) all-reduce(f32[128,8]{0,1:T(8,128)S(1)} %fusion.54, f32[128]{0:T(128)S(1)} %multiply_reduce_fusion), channel_id=1, replica_groups=mesh['groups'=2,'ctx'=4,'exp'=2,'tp'=2] {'exp','tp'}, use_global_device_ids=true, to_apply=%region_5.6 | all-reduce | flops 1152 | bytes 9216 | tf_op jit(solution)/shard_map/psum | solution.py:68
  26.6 0.6 reduce-window.6
  27.2 0.2 slice_reduce_fusion
  27.5 0.1 reduce_sum.57
  27.9 0.4 convolution_convert_fusion
  28.3 0.9 slice_bitcast_fusion
  29.1 5.2 %all-to-all-start = ((bf16[4,48,768]{2,1,0:T(8,128)(2,1)}), bf16[4,48,768]{2,1,0:T(8,128)(2,1)S(1)}, u32[]{:S(2)}, u32[]{:S(2)}) async-start(bf16[4,48,768]{2,1,0:T(8,128)(2,1)} %get-tuple-element.8), calls=%async_computation | async-start | bytes 589824 | tf_op jit(solution)/shard_map/all_to_all | solution.py:102
  34.4 9.6 %all-to-all-done = bf16[4,48,768]{2,1,0:T(8,128)(2,1)S(1)} async-done(((bf16[4,48,768]{2,1,0:T(8,128)(2,1)}), bf16[4,48,768]{2,1,0:T(8,128)(2,1)S(1)}, u32[]{:S(2)}, u32[]{:S(2)}) %all-to-all-start) | async-done | bytes 294944 | tf_op jit(solution)/shard_map/all_to_all | solution.py:102
  43.9 3.5 %all-to-all-start.2 = ((bf16[4,48,768]{2,1,0:T(8,128)(2,1)}), bf16[4,48,768]{2,1,0:T(8,128)(2,1)S(1)}, u32[]{:S(2)}, u32[]{:S(2)}) async-start(bf16[4,48,768]{2,1,0:T(8,128)(2,1)} %get-tuple-element.7), calls=%async_computation.2 | async-start | bytes 589824 | tf_op jit(solution)/shard_map/all_to_all | solution.py:102
  47.4 2.2 %all_gather.10 = bf16[192,1536]{1,0:T(8,128)(2,1)S(1)} all-gather(bf16[192,768]{1,0:T(8,128)(2,1)S(1)} %bitcast.88), channel_id=1, replica_groups=mesh['groups'=2,'ctx'=4,'exp'=2,'tp'=2] {'tp'}, dimensions={1}, use_global_device_ids=true | all-gather | bytes 884736 | tf_op jit(solution)/shard_map/all_gather | solution.py:104
  49.6 4.3 %fusion.33 = bf16[192,2048]{1,0:T(8,128)(2,1)S(1)} fusion(bf16[192,1536]{1,0:T(8,128)(2,1)S(1)} %all_gather.10, bf16[1536,1,8192]{2,0,1:T(8,128)(2,1)} %param.16), kind=kOutput, calls=%fused_computation.27 | convolution fusion | flops 1208352768 | bytes 7667712 | tf_op jit(solution)/shard_map/dot_general | solution.py:110
  53.9 4.3 %fusion.30 = bf16[192,2048]{1,0:T(8,128)(2,1)S(1)} fusion(bf16[192,1536]{1,0:T(8,128)(2,1)S(1)} %all_gather.10, bf16[1536,1,8192]{2,0,1:T(8,128)(2,1)} %param.16), kind=kOutput, calls=%fused_computation.26 | convolution fusion | flops 1208352768 | bytes 7667712 | tf_op jit(solution)/shard_map/dot_general | solution.py:110
  58.2 2.4 %all_gather.11 = bf16[192,1536]{1,0:T(8,128)(2,1)S(1)} all-gather(bf16[192,768]{1,0:T(8,128)(2,1)S(1)} %bitcast.89), channel_id=1, replica_groups=mesh['groups'=2,'ctx'=4,'exp'=2,'tp'=2] {'tp'}, dimensions={1}, use_global_device_ids=true | all-gather | bytes 884736 | tf_op jit(solution)/shard_map/all_gather | solution.py:104
  60.6 1.5 collective-permute-start.1
  62.1 4.3 %fusion.39 = bf16[192,2048]{1,0:T(8,128)(2,1)S(1)} fusion(bf16[192,1536]{1,0:T(8,128)(2,1)S(1)} %all_gather.11, bf16[1536,1,8192]{2,0,1:T(8,128)(2,1)} %param.16), kind=kOutput, calls=%fused_computation.29 | convolution fusion | flops 1208352768 | bytes 7667712 | tf_op jit(solution)/shard_map/dot_general | solution.py:110
  66.4 0.6 collective-permute-start
  67.0 4.4 %fusion.36 = bf16[192,2048]{1,0:T(8,128)(2,1)S(1)} fusion(bf16[192,1536]{1,0:T(8,128)(2,1)S(1)} %all_gather.11, bf16[1536,1,8192]{2,0,1:T(8,128)(2,1)} %param.16), kind=kOutput, calls=%fused_computation.28 | convolution fusion | flops 1208352768 | bytes 7667712 | tf_op jit(solution)/shard_map/dot_general | solution.py:110
  71.5 1.5 collective-permute-start.4
  73.0 0.6 collective-permute-start.3
  73.6 7.4 %collective-permute-done.1 = bf16[192,2048]{1,0:T(8,128)(2,1)S(1)} collective-permute-done((bf16[192,2048]{1,0:T(8,128)(2,1)S(1)}, bf16[192,2048]{1,0:T(8,128)(2,1)S(1)}, u32[]{:S(2)}, u32[]{:S(2)}) %collective-permute-start.1) | collective-permute-done | bytes 786464 | tf_op jit(solution)/shard_map/ppermute | solution.py:118
  81.0 4.2 %fusion.8 = f32[192,1536]{1,0:T(8,128)S(1)} fusion(bf16[1,8192,1536]{2,1,0:T(8,128)(2,1)} %param.17, bf16[192,2048]{1,0:T(8,128)(2,1)S(1)} %collective-permute-done.1, bf16[192,2048]{1,0:T(8,128)(2,1)S(1)} %fusion.33), kind=kOutput, calls=%fused_computation.8 | convolution fusion | flops 1211105280 | bytes 9043968 | tf_op jit(solution)/shard_map/dot_general | solution.py:128
  85.3 12.6 %collective-permute-done = bf16[192,2048]{1,0:T(8,128)(2,1)S(1)} collective-permute-done((bf16[192,2048]{1,0:T(8,128)(2,1)S(1)}, bf16[192,2048]{1,0:T(8,128)(2,1)S(1)}, u32[]{:S(2)}, u32[]{:S(2)}) %collective-permute-start) | collective-permute-done | bytes 786464 | tf_op jit(solution)/shard_map/ppermute | solution.py:118
  97.9 4.2 %fusion.24 = f32[192,1536]{1,0:T(8,128)S(1)} fusion(f32[192,1536]{1,0:T(8,128)S(1)} %fusion.8, bf16[1,8192,1536]{2,1,0:T(8,128)(2,1)} %param.17, bf16[192,2048]{1,0:T(8,128)(2,1)S(1)} %collective-permute-done, bf16[192,2048]{1,0:T(8,128)(2,1)S(1)} %fusion.30), kind=kOutput, calls=%fused_computation.24 | convolution fusion | flops 1211400192 | bytes 10223616 | tf_op jit(solution)/shard_map/dot_general | solution.py:128
  102.3 12.5 %collective-permute-done.4 = bf16[192,2048]{1,0:T(8,128)(2,1)S(1)} collective-permute-done((bf16[192,2048]{1,0:T(8,128)(2,1)S(1)}, bf16[192,2048]{1,0:T(8,128)(2,1)S(1)}, u32[]{:S(2)}, u32[]{:S(2)}) %collective-permute-start.4) | collective-permute-done | bytes 786464 | tf_op jit(solution)/shard_map/ppermute | solution.py:118
  114.8 1.4 fusion
  116.2 14.6 %collective-permute-done.3 = bf16[192,2048]{1,0:T(8,128)(2,1)S(1)} collective-permute-done((bf16[192,2048]{1,0:T(8,128)(2,1)S(1)}, bf16[192,2048]{1,0:T(8,128)(2,1)S(1)}, u32[]{:S(2)}, u32[]{:S(2)}) %collective-permute-start.3) | collective-permute-done | bytes 786464 | tf_op jit(solution)/shard_map/ppermute | solution.py:118
  130.8 1.4 fusion.27
  132.4 0.8 add_convert_fusion.1
  133.2 5.0 %all-to-all-start.1 = ((bf16[4,48,768]{2,1,0:T(8,128)(2,1)}), bf16[4,48,768]{2,1,0:T(8,128)(2,1)S(1)}, u32[]{:S(2)}, u32[]{:S(2)}) async-start(bf16[4,48,768]{2,1,0:T(8,128)(2,1)} %bitcast.18), calls=%async_computation.1 | async-start | bytes 589824 | tf_op jit(solution)/shard_map/all_to_all | solution.py:136
  138.2 0.1 select_reduce_fusion
  138.5 0.8 add_convert_fusion
  139.3 9.1 %all-to-all-done.1 = bf16[4,48,768]{2,1,0:T(8,128)(2,1)S(1)} async-done(((bf16[4,48,768]{2,1,0:T(8,128)(2,1)}), bf16[4,48,768]{2,1,0:T(8,128)(2,1)S(1)}, u32[]{:S(2)}, u32[]{:S(2)}) %all-to-all-start.1) | async-done | bytes 294944 | tf_op jit(solution)/shard_map/all_to_all | solution.py:136
  148.5 3.6 %all-to-all-start.3 = ((bf16[4,48,768]{2,1,0:T(8,128)(2,1)}), bf16[4,48,768]{2,1,0:T(8,128)(2,1)S(1)}, u32[]{:S(2)}, u32[]{:S(2)}) async-start(bf16[4,48,768]{2,1,0:T(8,128)(2,1)} %bitcast.27), calls=%async_computation.3 | async-start | bytes 589824 | tf_op jit(solution)/shard_map/all_to_all | solution.py:136
  152.1 0.4 fusion.68
  152.4 8.2 %all-to-all-done.3 = bf16[4,48,768]{2,1,0:T(8,128)(2,1)S(1)} async-done(((bf16[4,48,768]{2,1,0:T(8,128)(2,1)}), bf16[4,48,768]{2,1,0:T(8,128)(2,1)S(1)}, u32[]{:S(2)}, u32[]{:S(2)}) %all-to-all-start.3) | async-done | bytes 294944 | tf_op jit(solution)/shard_map/all_to_all | solution.py:136
  160.6 1.1 fusion.46
  (47 shorter events, 1.0 us)
Async XLA Ops:
  0.0 20.4 %copy-start = (f32[768,8]{0,1:T(8,128)S(1)}, f32[768,8]{0,1:T(8,128)}, u32[]{:S(2)}) copy-start(f32[768,8]{0,1:T(8,128)} %param.14) | copy-start | bytes 73732
  19.3 0.9 copy-start.2
  19.3 1.1 copy-start.3
  19.7 8.0 %copy-start.4 = (s32[128,2]{0,1:T(2,128)S(1)}, s32[128,2]{0,1:T(2,128)}, u32[]{:S(2)}) copy-start(s32[128,2]{0,1:T(2,128)} %param.15) | copy-start | bytes 3076
  29.1 14.8 %all-to-all-start = ((bf16[4,48,768]{2,1,0:T(8,128)(2,1)}), bf16[4,48,768]{2,1,0:T(8,128)(2,1)S(1)}, u32[]{:S(2)}, u32[]{:S(2)}) async-start(bf16[4,48,768]{2,1,0:T(8,128)(2,1)} %get-tuple-element.8), calls=%async_computation | async-start | bytes 589824 | tf_op jit(solution)/shard_map/all_to_all | solution.py:102
  43.9 14.3 %all-to-all-start.2 = ((bf16[4,48,768]{2,1,0:T(8,128)(2,1)}), bf16[4,48,768]{2,1,0:T(8,128)(2,1)S(1)}, u32[]{:S(2)}, u32[]{:S(2)}) async-start(bf16[4,48,768]{2,1,0:T(8,128)(2,1)} %get-tuple-element.7), calls=%async_computation.2 | async-start | bytes 589824 | tf_op jit(solution)/shard_map/all_to_all | solution.py:102
  60.6 20.4 %collective-permute-start.1 = (bf16[192,2048]{1,0:T(8,128)(2,1)S(1)}, bf16[192,2048]{1,0:T(8,128)(2,1)S(1)}, u32[]{:S(2)}, u32[]{:S(2)}) collective-permute-start(bf16[192,2048]{1,0:T(8,128)(2,1)S(1)} %fusion.33), channel_id=1, source_target_pairs={{0,2},{2,0},{1,3},{3,1},{4,6},{6,4},{5,7},{7,5},{8,10},{10,8},{9,1... | collective-permute-start | bytes 2359304 | tf_op jit(solution)/shard_map/ppermute | solution.py:118
  66.4 31.5 %collective-permute-start = (bf16[192,2048]{1,0:T(8,128)(2,1)S(1)}, bf16[192,2048]{1,0:T(8,128)(2,1)S(1)}, u32[]{:S(2)}, u32[]{:S(2)}) collective-permute-start(bf16[192,2048]{1,0:T(8,128)(2,1)S(1)} %fusion.30), channel_id=1, source_target_pairs={{0,2},{2,0},{1,3},{3,1},{4,6},{6,4},{5,7},{7,5},{8,10},{10,8},{9,1... | collective-permute-start | bytes 2359304 | tf_op jit(solution)/shard_map/ppermute | solution.py:118
  67.0 47.7 %slice-start = ((s8[25165824]{0:T(1024)(128)(4,1)}), s8[4194304]{0:T(1024)(128)(4,1)S(1)}, s32[]{:S(2)}) async-start(s8[25165824]{0:T(1024)(128)(4,1)} %bitcast.97), calls=%async_computation.4 | async-start | bytes 8388608
  67.0 47.7 %slice-start.1 = ((s8[25165824]{0:T(1024)(128)(4,1)}), s8[4194304]{0:T(1024)(128)(4,1)S(1)}, s32[]{:S(2)}) async-start(s8[25165824]{0:T(1024)(128)(4,1)} %bitcast.97), calls=%async_computation.5 | async-start | bytes 8388608
  71.5 43.3 %slice-start.2 = ((s8[25165824]{0:T(1024)(128)(4,1)}), s8[4194304]{0:T(1024)(128)(4,1)S(1)}, s32[]{:S(2)}) async-start(s8[25165824]{0:T(1024)(128)(4,1)} %bitcast.97), calls=%async_computation.6 | async-start | bytes 8388608
  71.5 43.3 %slice-start.3 = ((s8[25165824]{0:T(1024)(128)(4,1)}), s8[4194304]{0:T(1024)(128)(4,1)S(1)}, s32[]{:S(2)}) async-start(s8[25165824]{0:T(1024)(128)(4,1)} %bitcast.97), calls=%async_computation.7 | async-start | bytes 8388608
  71.5 43.2 %collective-permute-start.4 = (bf16[192,2048]{1,0:T(8,128)(2,1)S(1)}, bf16[192,2048]{1,0:T(8,128)(2,1)S(1)}, u32[]{:S(2)}, u32[]{:S(2)}) collective-permute-start(bf16[192,2048]{1,0:T(8,128)(2,1)S(1)} %fusion.39), channel_id=1, source_target_pairs={{0,2},{2,0},{1,3},{3,1},{4,6},{6,4},{5,7},{7,5},{8,10},{10,8},{9,1... | collective-permute-start | bytes 2359304 | tf_op jit(solution)/shard_map/ppermute | solution.py:118
  73.0 57.8 %collective-permute-start.3 = (bf16[192,2048]{1,0:T(8,128)(2,1)S(1)}, bf16[192,2048]{1,0:T(8,128)(2,1)S(1)}, u32[]{:S(2)}, u32[]{:S(2)}) collective-permute-start(bf16[192,2048]{1,0:T(8,128)(2,1)S(1)} %fusion.36), channel_id=1, source_target_pairs={{0,2},{2,0},{1,3},{3,1},{4,6},{6,4},{5,7},{7,5},{8,10},{10,8},{9,1... | collective-permute-start | bytes 2359304 | tf_op jit(solution)/shard_map/ppermute | solution.py:118
  85.3 29.5 %slice-start.4 = ((s8[25165824]{0:T(1024)(128)(4,1)}), s8[4194304]{0:T(1024)(128)(4,1)S(1)}, s32[]{:S(2)}) async-start(s8[25165824]{0:T(1024)(128)(4,1)} %bitcast.97), calls=%async_computation.8 | async-start | bytes 8388608
  85.3 29.5 %slice-start.5 = ((s8[25165824]{0:T(1024)(128)(4,1)}), s8[4194304]{0:T(1024)(128)(4,1)S(1)}, s32[]{:S(2)}) async-start(s8[25165824]{0:T(1024)(128)(4,1)} %bitcast.97), calls=%async_computation.9 | async-start | bytes 8388608
  102.2 30.2 %collective-permute-start.2 = (bf16[192,768]{1,0:T(8,128)(2,1)S(1)}, bf16[192,768]{1,0:T(8,128)(2,1)S(1)}, u32[]{:S(2)}, u32[]{:S(2)}) collective-permute-start(bf16[192,768]{1,0:T(8,128)(2,1)S(1)} %select_convert_fusion.1), channel_id=1, source_target_pairs={{0,1},{1,0},{2,3},{3,2},{4,5},{5,4},{6,7},{7,6},{8,9},{9,8},{10,11... | collective-permute-start | bytes 884744 | tf_op jit(solution)/shard_map/ppermute | solution.py:134
  132.3 6.2 %collective-permute-start.5 = (bf16[192,768]{1,0:T(8,128)(2,1)S(1)}, bf16[192,768]{1,0:T(8,128)(2,1)S(1)}, u32[]{:S(2)}, u32[]{:S(2)}) collective-permute-start(bf16[192,768]{1,0:T(8,128)(2,1)S(1)} %select_convert_fusion), channel_id=1, source_target_pairs={{0,1},{1,0},{2,3},{3,2},{4,5},{5,4},{6,7},{7,6},{8,9},{9,8},{10,11... | collective-permute-start | bytes 884744 | tf_op jit(solution)/shard_map/ppermute | solution.py:134
  133.2 15.3 %all-to-all-start.1 = ((bf16[4,48,768]{2,1,0:T(8,128)(2,1)}), bf16[4,48,768]{2,1,0:T(8,128)(2,1)S(1)}, u32[]{:S(2)}, u32[]{:S(2)}) async-start(bf16[4,48,768]{2,1,0:T(8,128)(2,1)} %bitcast.18), calls=%async_computation.1 | async-start | bytes 589824 | tf_op jit(solution)/shard_map/all_to_all | solution.py:136
  148.4 13.2 %copy-start.1 = (f32[768,8]{0,1:T(8,128)S(1)}, f32[768,8]{0,1:T(8,128)}, u32[]{:S(2)}) copy-start(f32[768,8]{0,1:T(8,128)} %param.14) | copy-start | bytes 73732
  148.5 12.2 %all-to-all-start.3 = ((bf16[4,48,768]{2,1,0:T(8,128)(2,1)}), bf16[4,48,768]{2,1,0:T(8,128)(2,1)S(1)}, u32[]{:S(2)}, u32[]{:S(2)}) async-start(bf16[4,48,768]{2,1,0:T(8,128)(2,1)} %bitcast.27), calls=%async_computation.3 | async-start | bytes 589824 | tf_op jit(solution)/shard_map/all_to_all | solution.py:136

commit v2 on v1

--- a/solution.py
+++ b/solution.py
@@ -10,7 +10,7 @@
 KVH = 4
 E = 8
 C = 48
-PIECES = 2
+PIECES = 4
 
 
 epsilon = 1e-05
@@ -47,9 +47,20 @@
         return lax.dynamic_slice_in_dim(rows, owner * HD, HD, axis=1)
 
     pair = jnp.concatenate([own_head(key_rows), own_head(value_rows)], axis=1)
-    pair = lax.all_gather(pair, "ctx", axis=0, tiled=True)
+    direct = ctx_count <= 4 and E % ctx_count == 0
+    if direct:
+        pieces_kv = [pair]
+        for shift in range(1, ctx_count):
+            later = [(j, j + shift) for j in range(ctx_count - shift)]
+            pieces_kv.append(lax.ppermute(pair, "ctx", later))
+        pair = jnp.concatenate(pieces_kv, axis=0)
+        column = jnp.arange(pair.shape[0], dtype=jnp.int32)
+        key_pos = first_row + column - 2 * (column // row_count) * row_count
+        visible = (query_pos[:, None] >= key_pos[None, :]) & (key_pos >= 0)[None, :]
+    else:
+        pair = lax.all_gather(pair, "ctx", axis=0, tiled=True)
+        visible = query_pos[:, None] >= jnp.arange(pair.shape[0], dtype=jnp.int32)[None, :]
     key_head, value_head = pair[:, :HD], pair[:, HD:]
-    visible = query_pos[:, None] >= jnp.arange(pair.shape[0], dtype=jnp.int32)[None, :]
     scores = jnp.einsum(
         "tqd,sd->qts", query_heads, key_head, preferred_element_type=jnp.float32
     ) * (1.0 / math.sqrt(HD))
@@ -65,10 +76,16 @@
     attended = jnp.transpose(accumulated / run_total, (1, 0, 2)).reshape(row_count, -1)
     mixed_in = residual.astype(jnp.float32) + attended
     scaled = mixed_in * norm_gain[None, :]
-    square_sum, logit_part = lax.psum(
-        (jnp.sum(mixed_in * mixed_in, axis=1), jnp.dot(scaled, router_weight, precision=highest)),
-        ("exp", "tp"),
-    )
+    square_sum = jnp.sum(mixed_in * mixed_in, axis=1)
+    logit_part = jnp.dot(scaled, router_weight, precision=highest)
+    ways = exp_count * tp_count
+    if ways == 4:
+        stats = jnp.concatenate([logit_part, square_sum[:, None]], axis=1).T
+        for flip in (1, 2):
+            stats = stats + lax.ppermute(stats, ("exp", "tp"), [(j, j ^ flip) for j in range(ways)])
+        logit_part, square_sum = stats[:E].T, stats[E]
+    else:
+        square_sum, logit_part = lax.psum((square_sum, logit_part), ("exp", "tp"))
     inv_rms = lax.rsqrt(square_sum / (QH * HD) + epsilon)
     moe_half = (scaled * inv_rms[:, None]).astype(jnp.bfloat16)
     logits = logit_part * inv_rms[:, None]
@@ -82,49 +99,73 @@
     flat_ids = expert_ids.reshape(-1)
     flat_hot = (flat_ids[:, None] == expert_range[None, :]).astype(jnp.int32)
     slot_index = jnp.sum((jnp.cumsum(flat_hot, axis=0) - flat_hot) * flat_hot, axis=1)
-    tile_row = (flat_ids * C + slot_index).reshape(row_count, 2)
+    ctx_sharing = max(1, ctx_count // E)
+    experts_held = max(1, E // ctx_count)
+    if direct:
+        away = (flat_ids // experts_held - lax.axis_index("ctx") + ctx_count) % ctx_count
+        tile_index = (flat_ids % experts_held) * ctx_count + away
+    else:
+        tile_index = (flat_ids % experts_held) * (E // experts_held) + flat_ids // experts_held
+    tile_row = (tile_index * C + slot_index).reshape(row_count, 2)
     tile_range = jnp.arange(E * C, dtype=jnp.int32)
     tile_hot = tile_row[:, :, None] == tile_range[None, None, :]
     combine_matrix = jnp.sum(jnp.where(tile_hot, gate_pair[:, :, None], 0.0), axis=1)
     dispatch_matrix = jnp.transpose(jnp.any(tile_hot, axis=1)).astype(jnp.bfloat16)
-    ctx_sharing = max(1, ctx_count // E)
-    experts_held = max(1, E // ctx_count)
     send_tiles = jnp.dot(dispatch_matrix, moe_half, preferred_element_type=jnp.float32).astype(
         jnp.bfloat16
     )
-    send_tiles = send_tiles.reshape(E, C, -1)
-    outgoing = jnp.repeat(send_tiles, ctx_sharing, axis=0).reshape(ctx_count, experts_held, C, -1)
+    send_tiles = send_tiles.reshape(experts_held, E // experts_held, C, -1)
+
+    def exchange(tiles, sign):
+        if not direct:
+            return lax.all_to_all(tiles, "ctx", split_axis=0, concat_axis=0, tiled=True)
+        moved = [tiles[0]]
+        for shift in range(1, ctx_count):
+            turned = [(j, (j + sign * shift) % ctx_count) for j in range(ctx_count)]
+            moved.append(lax.ppermute(tiles[shift], "ctx", turned))
+        return jnp.stack(moved)
+
     hidden_width = gate_weight.shape[2] // experts_held
     pieces = max(1, min(PIECES, hidden_width // 512))
     piece = hidden_width // pieces
-    arrived = []
-    for e in range(experts_held):
-        half = lax.all_to_all(outgoing[:, e], "ctx", split_axis=0, concat_axis=0, tiled=True)
-        arrived.append(
-            lax.all_gather(half.reshape(ctx_count * C, -1), "tp", axis=1, tiled=True)
-        )
+    halves = [
+        exchange(jnp.repeat(send_tiles[e], ctx_sharing, axis=0), 1).reshape(ctx_count * C, -1)
+        for e in range(experts_held)
+    ]
+    came = []
     sums = []
     for e in range(experts_held):
+        half = halves[e]
+        if came:
+            half, came[0] = lax.optimization_barrier((half, came[0]))
+        arrived = lax.all_gather(half, "tp", axis=1, tiled=True)
         for i in range(pieces):
             low = e * hidden_width + i * piece
+            if len(came) >= 2:
+                arrived, came[-2] = lax.optimization_barrier((arrived, came[-2]))
             part = jnp.dot(
-                arrived[e],
+                arrived,
                 gate_weight[:, 0, low : low + piece],
                 preferred_element_type=jnp.float32,
             ).astype(jnp.bfloat16)
-            total = part.astype(jnp.float32)
+            others = []
             for shift in range(1, exp_count):
                 turned = [(j, (j + shift) % exp_count) for j in range(exp_count)]
-                total = total + lax.ppermute(part, "exp", turned).astype(jnp.float32)
-            sums.append(total)
+                others.append(lax.ppermute(part, "exp", turned))
+            came.append(others)
+            sums.append(part)
+
+    def total_of(k):
+        return sum([p.astype(jnp.float32) for p in came[k]], sums[k].astype(jnp.float32))
+
     width_out = down_weight.shape[2] // tp_count
     moe_mine = 0.0
-    combine_parts = combine_matrix.reshape(row_count, -1, experts_held, C)
+    combine_parts = combine_matrix.reshape(row_count, experts_held, -1)
     for e in range(experts_held):
         out = 0.0
         for i in range(pieces):
             low = e * hidden_width + i * piece
-            hidden = jax.nn.silu(sums[e * pieces + i]).astype(jnp.bfloat16)
+            hidden = jax.nn.silu(total_of(e * pieces + i)).astype(jnp.bfloat16)
             out = out + jnp.dot(
                 hidden, down_weight[0, low : low + piece], preferred_element_type=jnp.float32
             )
@@ -133,16 +174,10 @@
         other = jnp.where(tp_index == 0, high_half, low_half).astype(jnp.bfloat16)
         swapped = lax.ppermute(other, "tp", [(0, 1), (1, 0)])
         core_summed = (mine + swapped.astype(jnp.float32)).astype(jnp.bfloat16)
-        returned = lax.all_to_all(
-            core_summed.reshape(ctx_count, C, width_out),
-            "ctx",
-            split_axis=0,
-            concat_axis=0,
-            tiled=True,
-        ).astype(jnp.float32)
+        returned = exchange(core_summed.reshape(ctx_count, C, width_out), -1).astype(jnp.float32)
         summed = jnp.sum(returned.reshape(-1, ctx_sharing, C, width_out), axis=1)
         moe_mine = moe_mine + jnp.dot(
-            combine_parts[:, :, e].reshape(row_count, -1),
+            combine_parts[:, e],
             summed.reshape(-1, width_out),
             precision=highest,
         )

time: 163 us -> 136 us (0.83)
  waiting for transfers between devices: 74 us -> 50.8 us
  blocking collectives: 26 us -> 4.62 us
  starting transfers between devices: 21.6 us -> 41.7 us
    ppermute x4 -> x25, starting transfers between devices: 4.18 us -> 41.5 us  [the longest x12 19.8 us: exchange(): moved.append(lax.ppermute(tiles[shift], 'ctx', turned))]
    all_to_all x4 -> x0, waiting for transfers between devices: 26.9 us -> none  [the longest x2 17.3 us: per_device(): lax.all_to_all(core_summed.reshape(ctx_count, C, width_out), 'ctx', split...]
    all_to_all x4 -> x0, starting transfers between devices: 17.2 us -> none  [the longest x2 8.62 us: per_device(): lax.all_to_all(core_summed.reshape(ctx_count, C, width_out), 'ctx', split...]
    all_gather x3 -> x2, blocking collectives: 20.3 us -> 4.62 us  [per_device(): arrived = lax.all_gather(half, 'tp', axis=1, tiled=True)]
    psum x1 -> x0, blocking collectives: 5.76 us -> none  [per_device(): lax.psum((jnp.sum(mixed_in * mixed_in, axis=1), jnp.dot(scaled, router_we...]
    dot_general x7 -> x11, matrix products: 19.2 us -> 24.3 us  [the longest x8 22.4 us: per_device(): jnp.dot(arrived, gate_weight[:, 0, low:low + piece], preferred_element_ty...]
    dot_general x4 -> x8, matrix products: 11.3 us -> 6.45 us  [per_device(): jnp.dot(hidden, down_weight[0, low:low + piece], preferred_element_type=j...]
    ppermute x4 -> x25, waiting for transfers between devices: 47.1 us -> 50.8 us  [the longest x8 39.2 us: per_device(): others.append(lax.ppermute(part, 'exp', turned))]
  transfers between devices with their start and end apart: 10 -> 27, of which waited for: 7 -> 14; matrix products, arithmetic and copies ran while one was open for 19% -> 25% of each run, Pallas kernels for 0% -> 0%
where the time goes in v2:
time: 136 us; the launch traced here: 135 us
  waiting for transfers between devices  50.8 us (37%)
  starting transfers between devices  41.7 us (31%)
  matrix products  31.9 us (23%)
  blocking collectives  4.62 us (3%)
  local copies, waits for them, and re-layouts  3.76 us (3%)
  other arithmetic  2.11 us (2%)
    ppermute x8, waiting for transfers between devices, per_device(): others.append(lax.ppermute(part, 'exp', turned))  39.2 us
    dot_general x8, matrix products, per_device(): jnp.dot(arrived, gate_weight[:, 0, low:low + piece], preferred_element_ty...  22.4 us
    ppermute x12, starting transfers between devices, exchange(): moved.append(lax.ppermute(tiles[shift], 'ctx', turned))  19.8 us
    ppermute x3, starting transfers between devices, per_device(): pieces_kv.append(lax.ppermute(pair, 'ctx', later))  10.7 us
    ppermute x8, starting transfers between devices, per_device(): others.append(lax.ppermute(part, 'exp', turned))  9.47 us
    ppermute x12, waiting for transfers between devices, exchange(): moved.append(lax.ppermute(tiles[shift], 'ctx', turned))  8.36 us
    dot_general x8, matrix products, per_device(): jnp.dot(hidden, down_weight[0, low:low + piece], preferred_element_type=j...  6.45 us
    all_gather x2, blocking collectives, per_device(): arrived = lax.all_gather(half, 'tp', axis=1, tiled=True)  4.62 us
  transfers between devices with their start and end apart: 27, of which 14 were waited for; matrix products, arithmetic and copies ran while one was open for 25% of the time, Pallas kernels for 0%

profile of v2, /device:TPU:0, one launch (start us, length us, event | category | flops | bytes accessed | tf_op | source)
XLA Modules:
  0.0 135.4 jit_solution(13716056055283940758)
XLA Ops:
  0.8 4.9 %collective-permute-start = (bf16[128,256]{1,0:T(8,128)(2,1)S(1)}, bf16[128,256]{1,0:T(8,128)(2,1)S(1)}, u32[]{:S(2)}, u32[]{:S(2)}) collective-permute-start(bf16[128,256]{1,0:T(8,128)(2,1)S(1)} %pad_maximum_fusion.5), channel_id=1, source_target_pairs={{0,4},{4,8},{8,12},{1,5},{5,9},{9,13},{2,6},{6,10},{10,14},{3,7},{... | collective-permute-start | bytes 196616 | tf_op jit(solution)/shard_map/ppermute | solution.py:55
  5.7 4.5 %collective-permute-start.1 = (bf16[128,256]{1,0:T(8,128)(2,1)S(1)}, bf16[128,256]{1,0:T(8,128)(2,1)S(1)}, u32[]{:S(2)}, u32[]{:S(2)}) collective-permute-start(bf16[128,256]{1,0:T(8,128)(2,1)S(1)} %pad_maximum_fusion.5), channel_id=1, source_target_pairs={{0,8},{4,12},{1,9},{5,13},{2,10},{6,14},{3,11},{7,15},{16,24},{20,... | collective-permute-start | bytes 196616 | tf_op jit(solution)/shard_map/ppermute | solution.py:55
  10.2 1.3 collective-permute-start.2
  12.7 1.1 copy.66
  17.1 1.1 collective-permute-done.3
  18.2 1.5 %collective-permute-start.4 = (f32[9,128]{1,0:T(8,128)S(1)}, f32[9,128]{1,0:T(8,128)S(1)}, u32[]{:S(2)}, u32[]{:S(2)}) collective-permute-start(f32[9,128]{1,0:T(8,128)S(1)} %fusion.127), channel_id=1, source_target_pairs={{0,2},{1,3},{2,0},{3,1},{4,6},{5,7},{6,4},{7,5},{8,10},{9,11},{10,... | collective-permute-start | bytes 13832 | tf_op jit(solution)/shard_map/ppermute | solution.py:85
  19.8 2.0 %collective-permute-done.4 = f32[9,128]{1,0:T(8,128)S(1)} collective-permute-done((f32[9,128]{1,0:T(8,128)S(1)}, f32[9,128]{1,0:T(8,128)S(1)}, u32[]{:S(2)}, u32[]{:S(2)}) %collective-permute-start.4) | collective-permute-done | bytes 4640 | tf_op jit(solution)/shard_map/ppermute | solution.py:85
  22.4 3.0 %collective-permute-start.6 = (bf16[48,768]{1,0:T(8,128)(2,1)S(1)}, bf16[48,768]{1,0:T(8,128)(2,1)S(1)}, u32[]{:S(2)}, u32[]{:S(2)}) collective-permute-start(bf16[48,768]{1,0:T(8,128)(2,1)S(1)} %get-tuple-element.39), channel_id=1, source_target_pairs={{0,8},{4,12},{8,0},{12,4},{1,9},{5,13},{9,1},{13,5},{2,10},{6,14},... | collective-permute-start | bytes 221192 | tf_op jit(solution)/shard_map/ppermute | solution.py:125
  25.4 0.8 collective-permute-start.7
  26.2 1.2 collective-permute-start.8
  27.4 0.8 collective-permute-start.9
  29.0 2.6 %collective-permute-start.10 = (bf16[48,768]{1,0:T(8,128)(2,1)S(1)}, bf16[48,768]{1,0:T(8,128)(2,1)S(1)}, u32[]{:S(2)}, u32[]{:S(2)}) collective-permute-start(bf16[48,768]{1,0:T(8,128)(2,1)S(1)} %get-tuple-element.34), channel_id=1, source_target_pairs={{0,12},{4,0},{8,4},{12,8},{1,13},{5,1},{9,5},{13,9},{2,14},{6,2},{... | collective-permute-start | bytes 221192 | tf_op jit(solution)/shard_map/ppermute | solution.py:125
  31.9 2.2 %all_gather.6 = bf16[192,1536]{1,0:T(8,128)(2,1)S(1)} all-gather(bf16[192,768]{1,0:T(8,128)(2,1)S(1)} %bitcast.155), channel_id=1, replica_groups=mesh['groups'=2,'ctx'=4,'exp'=2,'tp'=2] {'tp'}, dimensions={1}, use_global_device_ids=true | all-gather | bytes 884736 | tf_op jit(solution)/shard_map/all_gather | solution.py:141
  34.2 2.9 %fusion.68 = bf16[192,1024]{1,0:T(8,128)(2,1)S(1)} fusion(bf16[192,1536]{1,0:T(8,128)(2,1)S(1)} %all_gather.6, bf16[1536,1,8192]{2,0,1:T(8,128)(2,1)} %param.16), kind=kOutput, calls=%fused_computation.59 | convolution fusion | flops 604176384 | bytes 4128768 | tf_op jit(solution)/shard_map/dot_general | solution.py:146
  37.1 1.6 %collective-permute-start.11 = (bf16[192,1024]{1,0:T(8,128)(2,1)S(1)}, bf16[192,1024]{1,0:T(8,128)(2,1)S(1)}, u32[]{:S(2)}, u32[]{:S(2)}) collective-permute-start(bf16[192,1024]{1,0:T(8,128)(2,1)S(1)} %fusion.68), channel_id=1, source_target_pairs={{0,2},{2,0},{1,3},{3,1},{4,6},{6,4},{5,7},{7,5},{8,10},{10,8},{9,1... | collective-permute-start | bytes 1179656 | tf_op jit(solution)/shard_map/ppermute | solution.py:154
  38.6 3.5 %fusion.71 = bf16[192,1024]{1,0:T(8,128)(2,1)S(1)} fusion(bf16[192,1536]{1,0:T(8,128)(2,1)S(1)} %all_gather.6, bf16[1536,1,8192]{2,0,1:T(8,128)(2,1)} %param.16), kind=kOutput, calls=%fused_computation.60 | convolution fusion | flops 604176384 | bytes 4128768 | tf_op jit(solution)/shard_map/dot_general | solution.py:146
  42.7 6.3 %collective-permute-done.11 = bf16[192,1024]{1,0:T(8,128)(2,1)S(1)} collective-permute-done((bf16[192,1024]{1,0:T(8,128)(2,1)S(1)}, bf16[192,1024]{1,0:T(8,128)(2,1)S(1)}, u32[]{:S(2)}, u32[]{:S(2)}) %collective-permute-start.11) | collective-permute-done | bytes 393248 | tf_op jit(solution)/shard_map/ppermute | solution.py:154
  49.1 2.7 %fusion.74 = bf16[192,1024]{1,0:T(8,128)(2,1)S(1)} fusion(bf16[192,1536]{1,0:T(8,128)(2,1)S(1)} %all_gather.6, bf16[1536,1,8192]{2,0,1:T(8,128)(2,1)} %param.16), kind=kOutput, calls=%fused_computation.61 | convolution fusion | flops 604176384 | bytes 4128768 | tf_op jit(solution)/shard_map/dot_general | solution.py:146
  51.8 1.6 %collective-permute-start.13 = (bf16[192,1024]{1,0:T(8,128)(2,1)S(1)}, bf16[192,1024]{1,0:T(8,128)(2,1)S(1)}, u32[]{:S(2)}, u32[]{:S(2)}) collective-permute-start(bf16[192,1024]{1,0:T(8,128)(2,1)S(1)} %fusion.74), channel_id=1, source_target_pairs={{0,2},{2,0},{1,3},{3,1},{4,6},{6,4},{5,7},{7,5},{8,10},{10,8},{9,1... | collective-permute-start | bytes 1179656 | tf_op jit(solution)/shard_map/ppermute | solution.py:154
  53.4 2.4 %all_gather.7 = bf16[192,1536]{1,0:T(8,128)(2,1)S(1)} all-gather(bf16[192,768]{1,0:T(8,128)(2,1)S(1)} %bitcast.154), channel_id=1, replica_groups=mesh['groups'=2,'ctx'=4,'exp'=2,'tp'=2] {'tp'}, dimensions={1}, use_global_device_ids=true | all-gather | bytes 884736 | tf_op jit(solution)/shard_map/all_gather | solution.py:141
  55.8 1.7 %collective-permute-done.12 = bf16[192,1024]{1,0:T(8,128)(2,1)S(1)} collective-permute-done((bf16[192,1024]{1,0:T(8,128)(2,1)S(1)}, bf16[192,1024]{1,0:T(8,128)(2,1)S(1)}, u32[]{:S(2)}, u32[]{:S(2)}) %collective-permute-start.12) | collective-permute-done | bytes 393248 | tf_op jit(solution)/shard_map/ppermute | solution.py:154
  57.5 2.7 %fusion.77 = bf16[192,1024]{1,0:T(8,128)(2,1)S(1)} fusion(bf16[192,1536]{1,0:T(8,128)(2,1)S(1)} %all_gather.6, bf16[1536,1,8192]{2,0,1:T(8,128)(2,1)} %param.16), kind=kOutput, calls=%fused_computation.62 | convolution fusion | flops 604176384 | bytes 4128768 | tf_op jit(solution)/shard_map/dot_general | solution.py:146
  60.2 1.6 %collective-permute-start.14 = (bf16[192,1024]{1,0:T(8,128)(2,1)S(1)}, bf16[192,1024]{1,0:T(8,128)(2,1)S(1)}, u32[]{:S(2)}, u32[]{:S(2)}) collective-permute-start(bf16[192,1024]{1,0:T(8,128)(2,1)S(1)} %fusion.77), channel_id=1, source_target_pairs={{0,2},{2,0},{1,3},{3,1},{4,6},{6,4},{5,7},{7,5},{8,10},{10,8},{9,1... | collective-permute-start | bytes 1179656 | tf_op jit(solution)/shard_map/ppermute | solution.py:154
  62.6 3.3 %collective-permute-done.13 = bf16[192,1024]{1,0:T(8,128)(2,1)S(1)} collective-permute-done((bf16[192,1024]{1,0:T(8,128)(2,1)S(1)}, bf16[192,1024]{1,0:T(8,128)(2,1)S(1)}, u32[]{:S(2)}, u32[]{:S(2)}) %collective-permute-start.13) | collective-permute-done | bytes 393248 | tf_op jit(solution)/shard_map/ppermute | solution.py:154
  65.9 2.7 %fusion.80 = bf16[192,1024]{1,0:T(8,128)(2,1)S(1)} fusion(bf16[192,1536]{1,0:T(8,128)(2,1)S(1)} %all_gather.7, bf16[1536,1,8192]{2,0,1:T(8,128)(2,1)} %param.16), kind=kOutput, calls=%fused_computation.63 | convolution fusion | flops 604176384 | bytes 4128768 | tf_op jit(solution)/shard_map/dot_general | solution.py:146
  68.6 0.8 fusion.20
  69.4 4.1 %collective-permute-done.14 = bf16[192,1024]{1,0:T(8,128)(2,1)S(1)} collective-permute-done((bf16[192,1024]{1,0:T(8,128)(2,1)S(1)}, bf16[192,1024]{1,0:T(8,128)(2,1)S(1)}, u32[]{:S(2)}, u32[]{:S(2)}) %collective-permute-start.14) | collective-permute-done | bytes 393248 | tf_op jit(solution)/shard_map/ppermute | solution.py:154
  73.6 1.5 %collective-permute-start.19 = (bf16[192,1024]{1,0:T(8,128)(2,1)S(1)}, bf16[192,1024]{1,0:T(8,128)(2,1)S(1)}, u32[]{:S(2)}, u32[]{:S(2)}) collective-permute-start(bf16[192,1024]{1,0:T(8,128)(2,1)S(1)} %fusion.80), channel_id=1, source_target_pairs={{0,2},{2,0},{1,3},{3,1},{4,6},{6,4},{5,7},{7,5},{8,10},{10,8},{9,1... | collective-permute-start | bytes 1179656 | tf_op jit(solution)/shard_map/ppermute | solution.py:154
  75.1 2.7 %fusion.83 = bf16[192,1024]{1,0:T(8,128)(2,1)S(1)} fusion(bf16[192,1536]{1,0:T(8,128)(2,1)S(1)} %all_gather.7, bf16[1536,1,8192]{2,0,1:T(8,128)(2,1)} %param.16), kind=kOutput, calls=%fused_computation.64 | convolution fusion | flops 604176384 | bytes 4128768 | tf_op jit(solution)/shard_map/dot_general | solution.py:146
  78.3 0.8 fusion.51
  79.1 0.8 fusion.54
  80.1 5.5 %collective-permute-done.19 = bf16[192,1024]{1,0:T(8,128)(2,1)S(1)} collective-permute-done((bf16[192,1024]{1,0:T(8,128)(2,1)S(1)}, bf16[192,1024]{1,0:T(8,128)(2,1)S(1)}, u32[]{:S(2)}, u32[]{:S(2)}) %collective-permute-start.19) | collective-permute-done | bytes 393248 | tf_op jit(solution)/shard_map/ppermute | solution.py:154
  85.6 2.7 %fusion.86 = bf16[192,1024]{1,0:T(8,128)(2,1)S(1)} fusion(bf16[192,1536]{1,0:T(8,128)(2,1)S(1)} %all_gather.7, bf16[1536,1,8192]{2,0,1:T(8,128)(2,1)} %param.16), kind=kOutput, calls=%fused_computation.65 | convolution fusion | flops 604176384 | bytes 4128768 | tf_op jit(solution)/shard_map/dot_general | solution.py:146
  88.3 4.0 %collective-permute-done.20 = bf16[192,1024]{1,0:T(8,128)(2,1)S(1)} collective-permute-done((bf16[192,1024]{1,0:T(8,128)(2,1)S(1)}, bf16[192,1024]{1,0:T(8,128)(2,1)S(1)}, u32[]{:S(2)}, u32[]{:S(2)}) %collective-permute-start.20) | collective-permute-done | bytes 393248 | tf_op jit(solution)/shard_map/ppermute | solution.py:154
  92.3 0.8 fusion.8
  93.1 2.7 %fusion.89 = bf16[192,1024]{1,0:T(8,128)(2,1)S(1)} fusion(bf16[192,1536]{1,0:T(8,128)(2,1)S(1)} %all_gather.7, bf16[1536,1,8192]{2,0,1:T(8,128)(2,1)} %param.16), kind=kOutput, calls=%fused_computation.66 | convolution fusion | flops 604176384 | bytes 4128768 | tf_op jit(solution)/shard_map/dot_general | solution.py:146
  95.8 1.5 %collective-permute-start.22 = (bf16[192,1024]{1,0:T(8,128)(2,1)S(1)}, bf16[192,1024]{1,0:T(8,128)(2,1)S(1)}, u32[]{:S(2)}, u32[]{:S(2)}) collective-permute-start(bf16[192,1024]{1,0:T(8,128)(2,1)S(1)} %fusion.89), channel_id=1, source_target_pairs={{0,2},{2,0},{1,3},{3,1},{4,6},{6,4},{5,7},{7,5},{8,10},{10,8},{9,1... | collective-permute-start | bytes 1179656 | tf_op jit(solution)/shard_map/ppermute | solution.py:154
  97.9 0.8 fusion.57
  98.7 9.2 %collective-permute-done.22 = bf16[192,1024]{1,0:T(8,128)(2,1)S(1)} collective-permute-done((bf16[192,1024]{1,0:T(8,128)(2,1)S(1)}, bf16[192,1024]{1,0:T(8,128)(2,1)S(1)}, u32[]{:S(2)}, u32[]{:S(2)}) %collective-permute-start.22) | collective-permute-done | bytes 393248 | tf_op jit(solution)/shard_map/ppermute | solution.py:154
  108.7 5.0 %collective-permute-done.21 = bf16[192,1024]{1,0:T(8,128)(2,1)S(1)} collective-permute-done((bf16[192,1024]{1,0:T(8,128)(2,1)S(1)}, bf16[192,1024]{1,0:T(8,128)(2,1)S(1)}, u32[]{:S(2)}, u32[]{:S(2)}) %collective-permute-start.21) | collective-permute-done | bytes 393248 | tf_op jit(solution)/shard_map/ppermute | solution.py:154
  113.7 0.8 fusion.63
  114.8 4.5 %collective-permute-start.16 = (bf16[48,768]{1,0:T(8,128)(2,1)S(1)}, bf16[48,768]{1,0:T(8,128)(2,1)S(1)}, u32[]{:S(2)}, u32[]{:S(2)}) collective-permute-start(bf16[48,768]{1,0:T(8,128)(2,1)S(1)} %get-tuple-element.44), channel_id=1, source_target_pairs={{0,12},{4,0},{8,4},{12,8},{1,13},{5,1},{9,5},{13,9},{2,14},{6,2},{... | collective-permute-start | bytes 221192 | tf_op jit(solution)/shard_map/ppermute | solution.py:125
  119.3 1.0 collective-permute-start.17
  120.3 3.9 %collective-permute-start.24 = (bf16[48,768]{1,0:T(8,128)(2,1)S(1)}, bf16[48,768]{1,0:T(8,128)(2,1)S(1)}, u32[]{:S(2)}, u32[]{:S(2)}) collective-permute-start(bf16[48,768]{1,0:T(8,128)(2,1)S(1)} %get-tuple-element.48), channel_id=1, source_target_pairs={{0,12},{4,0},{8,4},{12,8},{1,13},{5,1},{9,5},{13,9},{2,14},{6,2},{... | collective-permute-start | bytes 221192 | tf_op jit(solution)/shard_map/ppermute | solution.py:125
  124.4 1.8 %collective-permute-start.26 = (bf16[48,768]{1,0:T(8,128)(2,1)S(1)}, bf16[48,768]{1,0:T(8,128)(2,1)S(1)}, u32[]{:S(2)}, u32[]{:S(2)}) collective-permute-start(bf16[48,768]{1,0:T(8,128)(2,1)S(1)} %get-tuple-element.46), channel_id=1, source_target_pairs={{0,4},{4,8},{8,12},{12,0},{1,5},{5,9},{9,13},{13,1},{2,6},{6,10},{... | collective-permute-start | bytes 221192 | tf_op jit(solution)/shard_map/ppermute | solution.py:125
  126.2 4.9 %collective-permute-done.17 = bf16[48,768]{1,0:T(8,128)(2,1)S(1)} collective-permute-done((bf16[48,768]{1,0:T(8,128)(2,1)S(1)}, bf16[48,768]{1,0:T(8,128)(2,1)S(1)}, u32[]{:S(2)}, u32[]{:S(2)}) %collective-permute-start.17) | collective-permute-done | bytes 73760 | tf_op jit(solution)/shard_map/ppermute | solution.py:125
  131.2 2.7 %collective-permute-done.25 = bf16[48,768]{1,0:T(8,128)(2,1)S(1)} collective-permute-done((bf16[48,768]{1,0:T(8,128)(2,1)S(1)}, bf16[48,768]{1,0:T(8,128)(2,1)S(1)}, u32[]{:S(2)}, u32[]{:S(2)}) %collective-permute-start.25) | collective-permute-done | bytes 73760 | tf_op jit(solution)/shard_map/ppermute | solution.py:125
  134.3 1.1 fusion.94
  (87 shorter events, 11.3 us)
Async XLA Ops:
  0.0 16.6 %copy-start = (f32[768,8]{0,1:T(8,128)S(1)}, f32[768,8]{0,1:T(8,128)}, u32[]{:S(2)}) copy-start(f32[768,8]{0,1:T(8,128)} %param.14) | copy-start | bytes 73732
  0.8 14.3 %collective-permute-start = (bf16[128,256]{1,0:T(8,128)(2,1)S(1)}, bf16[128,256]{1,0:T(8,128)(2,1)S(1)}, u32[]{:S(2)}, u32[]{:S(2)}) collective-permute-start(bf16[128,256]{1,0:T(8,128)(2,1)S(1)} %pad_maximum_fusion.5), channel_id=1, source_target_pairs={{0,4},{4,8},{8,12},{1,5},{5,9},{9,13},{2,6},{6,10},{10,14},{3,7},{... | collective-permute-start | bytes 196616 | tf_op jit(solution)/shard_map/ppermute | solution.py:55
  5.7 9.4 %collective-permute-start.1 = (bf16[128,256]{1,0:T(8,128)(2,1)S(1)}, bf16[128,256]{1,0:T(8,128)(2,1)S(1)}, u32[]{:S(2)}, u32[]{:S(2)}) collective-permute-start(bf16[128,256]{1,0:T(8,128)(2,1)S(1)} %pad_maximum_fusion.5), channel_id=1, source_target_pairs={{0,8},{4,12},{1,9},{5,13},{2,10},{6,14},{3,11},{7,15},{16,24},{20,... | collective-permute-start | bytes 196616 | tf_op jit(solution)/shard_map/ppermute | solution.py:55
  10.2 4.9 %collective-permute-start.2 = (bf16[128,256]{1,0:T(8,128)(2,1)S(1)}, bf16[128,256]{1,0:T(8,128)(2,1)S(1)}, u32[]{:S(2)}, u32[]{:S(2)}) collective-permute-start(bf16[128,256]{1,0:T(8,128)(2,1)S(1)} %pad_maximum_fusion.5), channel_id=1, source_target_pairs={{0,12},{1,13},{2,14},{3,15},{16,28},{17,29},{18,30},{19,31}} | collective-permute-start | bytes 196616 | tf_op jit(solution)/shard_map/ppermute | solution.py:55
  15.2 1.2 copy-start.2
  15.6 1.0 copy-start.3
  15.6 1.4 %copy-start.4 = (s32[128,2]{0,1:T(2,128)S(1)}, s32[128,2]{0,1:T(2,128)}, u32[]{:S(2)}) copy-start(s32[128,2]{0,1:T(2,128)} %param.15) | copy-start | bytes 3076
  17.0 1.2 collective-permute-start.3
  18.2 3.7 %collective-permute-start.4 = (f32[9,128]{1,0:T(8,128)S(1)}, f32[9,128]{1,0:T(8,128)S(1)}, u32[]{:S(2)}, u32[]{:S(2)}) collective-permute-start(f32[9,128]{1,0:T(8,128)S(1)} %fusion.127), channel_id=1, source_target_pairs={{0,2},{1,3},{2,0},{3,1},{4,6},{5,7},{6,4},{7,5},{8,10},{9,11},{10,... | collective-permute-start | bytes 13832 | tf_op jit(solution)/shard_map/ppermute | solution.py:85
  22.3 6.6 %collective-permute-start.5 = (bf16[48,768]{1,0:T(8,128)(2,1)S(1)}, bf16[48,768]{1,0:T(8,128)(2,1)S(1)}, u32[]{:S(2)}, u32[]{:S(2)}) collective-permute-start(bf16[48,768]{1,0:T(8,128)(2,1)S(1)} %get-tuple-element.40), channel_id=1, source_target_pairs={{0,4},{4,8},{8,12},{12,0},{1,5},{5,9},{9,13},{13,1},{2,6},{6,10},{... | collective-permute-start | bytes 221192 | tf_op jit(solution)/shard_map/ppermute | solution.py:125
  22.4 9.5 %collective-permute-start.6 = (bf16[48,768]{1,0:T(8,128)(2,1)S(1)}, bf16[48,768]{1,0:T(8,128)(2,1)S(1)}, u32[]{:S(2)}, u32[]{:S(2)}) collective-permute-start(bf16[48,768]{1,0:T(8,128)(2,1)S(1)} %get-tuple-element.39), channel_id=1, source_target_pairs={{0,8},{4,12},{8,0},{12,4},{1,9},{5,13},{9,1},{13,5},{2,10},{6,14},... | collective-permute-start | bytes 221192 | tf_op jit(solution)/shard_map/ppermute | solution.py:125
  25.4 6.5 %collective-permute-start.7 = (bf16[48,768]{1,0:T(8,128)(2,1)S(1)}, bf16[48,768]{1,0:T(8,128)(2,1)S(1)}, u32[]{:S(2)}, u32[]{:S(2)}) collective-permute-start(bf16[48,768]{1,0:T(8,128)(2,1)S(1)} %get-tuple-element.38), channel_id=1, source_target_pairs={{0,12},{4,0},{8,4},{12,8},{1,13},{5,1},{9,5},{13,9},{2,14},{6,2},{... | collective-permute-start | bytes 221192 | tf_op jit(solution)/shard_map/ppermute | solution.py:125
  26.2 16.5 %collective-permute-start.8 = (bf16[48,768]{1,0:T(8,128)(2,1)S(1)}, bf16[48,768]{1,0:T(8,128)(2,1)S(1)}, u32[]{:S(2)}, u32[]{:S(2)}) collective-permute-start(bf16[48,768]{1,0:T(8,128)(2,1)S(1)} %get-tuple-element.36), channel_id=1, source_target_pairs={{0,4},{4,8},{8,12},{12,0},{1,5},{5,9},{9,13},{13,1},{2,6},{6,10},{... | collective-permute-start | bytes 221192 | tf_op jit(solution)/shard_map/ppermute | solution.py:125
  27.4 15.3 %collective-permute-start.9 = (bf16[48,768]{1,0:T(8,128)(2,1)S(1)}, bf16[48,768]{1,0:T(8,128)(2,1)S(1)}, u32[]{:S(2)}, u32[]{:S(2)}) collective-permute-start(bf16[48,768]{1,0:T(8,128)(2,1)S(1)} %get-tuple-element.35), channel_id=1, source_target_pairs={{0,8},{4,12},{8,0},{12,4},{1,9},{5,13},{9,1},{13,5},{2,10},{6,14},... | collective-permute-start | bytes 221192 | tf_op jit(solution)/shard_map/ppermute | solution.py:125
  29.0 13.7 %collective-permute-start.10 = (bf16[48,768]{1,0:T(8,128)(2,1)S(1)}, bf16[48,768]{1,0:T(8,128)(2,1)S(1)}, u32[]{:S(2)}, u32[]{:S(2)}) collective-permute-start(bf16[48,768]{1,0:T(8,128)(2,1)S(1)} %get-tuple-element.34), channel_id=1, source_target_pairs={{0,12},{4,0},{8,4},{12,8},{1,13},{5,1},{9,5},{13,9},{2,14},{6,2},{... | collective-permute-start | bytes 221192 | tf_op jit(solution)/shard_map/ppermute | solution.py:125
  34.2 27.6 %copy-start.5 = (bf16[1,8192,1536]{2,1,0:T(8,128)(2,1)S(1)}, bf16[1,8192,1536]{2,1,0:T(8,128)(2,1)}, u32[]{:S(2)}) copy-start(bf16[1,8192,1536]{2,1,0:T(8,128)(2,1)} %param.17) | copy-start | bytes 75497472
  37.1 12.0 %collective-permute-start.11 = (bf16[192,1024]{1,0:T(8,128)(2,1)S(1)}, bf16[192,1024]{1,0:T(8,128)(2,1)S(1)}, u32[]{:S(2)}, u32[]{:S(2)}) collective-permute-start(bf16[192,1024]{1,0:T(8,128)(2,1)S(1)} %fusion.68), channel_id=1, source_target_pairs={{0,2},{2,0},{1,3},{3,1},{4,6},{6,4},{5,7},{7,5},{8,10},{10,8},{9,1... | collective-permute-start | bytes 1179656 | tf_op jit(solution)/shard_map/ppermute | solution.py:154
  42.1 15.4 %collective-permute-start.12 = (bf16[192,1024]{1,0:T(8,128)(2,1)S(1)}, bf16[192,1024]{1,0:T(8,128)(2,1)S(1)}, u32[]{:S(2)}, u32[]{:S(2)}) collective-permute-start(bf16[192,1024]{1,0:T(8,128)(2,1)S(1)} %fusion.71), channel_id=1, source_target_pairs={{0,2},{2,0},{1,3},{3,1},{4,6},{6,4},{5,7},{7,5},{8,10},{10,8},{9,1... | collective-permute-start | bytes 1179656 | tf_op jit(solution)/shard_map/ppermute | solution.py:154
  51.8 14.1 %collective-permute-start.13 = (bf16[192,1024]{1,0:T(8,128)(2,1)S(1)}, bf16[192,1024]{1,0:T(8,128)(2,1)S(1)}, u32[]{:S(2)}, u32[]{:S(2)}) collective-permute-start(bf16[192,1024]{1,0:T(8,128)(2,1)S(1)} %fusion.74), channel_id=1, source_target_pairs={{0,2},{2,0},{1,3},{3,1},{4,6},{6,4},{5,7},{7,5},{8,10},{10,8},{9,1... | collective-permute-start | bytes 1179656 | tf_op jit(solution)/shard_map/ppermute | solution.py:154
  60.2 13.3 %collective-permute-start.14 = (bf16[192,1024]{1,0:T(8,128)(2,1)S(1)}, bf16[192,1024]{1,0:T(8,128)(2,1)S(1)}, u32[]{:S(2)}, u32[]{:S(2)}) collective-permute-start(bf16[192,1024]{1,0:T(8,128)(2,1)S(1)} %fusion.77), channel_id=1, source_target_pairs={{0,2},{2,0},{1,3},{3,1},{4,6},{6,4},{5,7},{7,5},{8,10},{10,8},{9,1... | collective-permute-start | bytes 1179656 | tf_op jit(solution)/shard_map/ppermute | solution.py:154
  73.6 12.1 %collective-permute-start.19 = (bf16[192,1024]{1,0:T(8,128)(2,1)S(1)}, bf16[192,1024]{1,0:T(8,128)(2,1)S(1)}, u32[]{:S(2)}, u32[]{:S(2)}) collective-permute-start(bf16[192,1024]{1,0:T(8,128)(2,1)S(1)} %fusion.80), channel_id=1, source_target_pairs={{0,2},{2,0},{1,3},{3,1},{4,6},{6,4},{5,7},{7,5},{8,10},{10,8},{9,1... | collective-permute-start | bytes 1179656 | tf_op jit(solution)/shard_map/ppermute | solution.py:154
  77.7 14.6 %collective-permute-start.20 = (bf16[192,1024]{1,0:T(8,128)(2,1)S(1)}, bf16[192,1024]{1,0:T(8,128)(2,1)S(1)}, u32[]{:S(2)}, u32[]{:S(2)}) collective-permute-start(bf16[192,1024]{1,0:T(8,128)(2,1)S(1)} %fusion.83), channel_id=1, source_target_pairs={{0,2},{2,0},{1,3},{3,1},{4,6},{6,4},{5,7},{7,5},{8,10},{10,8},{9,1... | collective-permute-start | bytes 1179656 | tf_op jit(solution)/shard_map/ppermute | solution.py:154
  80.0 34.6 %collective-permute-start.15 = (bf16[192,768]{1,0:T(8,128)(2,1)S(1)}, bf16[192,768]{1,0:T(8,128)(2,1)S(1)}, u32[]{:S(2)}, u32[]{:S(2)}) collective-permute-start(bf16[192,768]{1,0:T(8,128)(2,1)S(1)} %select_convert_fusion.1), channel_id=1, source_target_pairs={{0,1},{1,0},{2,3},{3,2},{4,5},{5,4},{6,7},{7,6},{8,9},{9,8},{10,11... | collective-permute-start | bytes 884744 | tf_op jit(solution)/shard_map/ppermute | solution.py:175
  95.8 12.1 %collective-permute-start.22 = (bf16[192,1024]{1,0:T(8,128)(2,1)S(1)}, bf16[192,1024]{1,0:T(8,128)(2,1)S(1)}, u32[]{:S(2)}, u32[]{:S(2)}) collective-permute-start(bf16[192,1024]{1,0:T(8,128)(2,1)S(1)} %fusion.89), channel_id=1, source_target_pairs={{0,2},{2,0},{1,3},{3,1},{4,6},{6,4},{5,7},{7,5},{8,10},{10,8},{9,1... | collective-permute-start | bytes 1179656 | tf_op jit(solution)/shard_map/ppermute | solution.py:154
  97.4 16.3 %collective-permute-start.21 = (bf16[192,1024]{1,0:T(8,128)(2,1)S(1)}, bf16[192,1024]{1,0:T(8,128)(2,1)S(1)}, u32[]{:S(2)}, u32[]{:S(2)}) collective-permute-start(bf16[192,1024]{1,0:T(8,128)(2,1)S(1)} %fusion.86), channel_id=1, source_target_pairs={{0,2},{2,0},{1,3},{3,1},{4,6},{6,4},{5,7},{7,5},{8,10},{10,8},{9,1... | collective-permute-start | bytes 1179656 | tf_op jit(solution)/shard_map/ppermute | solution.py:154
  114.6 5.7 %collective-permute-start.23 = (bf16[192,768]{1,0:T(8,128)(2,1)S(1)}, bf16[192,768]{1,0:T(8,128)(2,1)S(1)}, u32[]{:S(2)}, u32[]{:S(2)}) collective-permute-start(bf16[192,768]{1,0:T(8,128)(2,1)S(1)} %select_convert_fusion), channel_id=1, source_target_pairs={{0,1},{1,0},{2,3},{3,2},{4,5},{5,4},{6,7},{7,6},{8,9},{9,8},{10,11... | collective-permute-start | bytes 884744 | tf_op jit(solution)/shard_map/ppermute | solution.py:175
  114.7 20.7 %copy-start.1 = (f32[768,8]{0,1:T(8,128)S(1)}, f32[768,8]{0,1:T(8,128)}, u32[]{:S(2)}) copy-start(f32[768,8]{0,1:T(8,128)} %param.14) | copy-start | bytes 73732
  114.8 9.6 %collective-permute-start.16 = (bf16[48,768]{1,0:T(8,128)(2,1)S(1)}, bf16[48,768]{1,0:T(8,128)(2,1)S(1)}, u32[]{:S(2)}, u32[]{:S(2)}) collective-permute-start(bf16[48,768]{1,0:T(8,128)(2,1)S(1)} %get-tuple-element.44), channel_id=1, source_target_pairs={{0,12},{4,0},{8,4},{12,8},{1,13},{5,1},{9,5},{13,9},{2,14},{6,2},{... | collective-permute-start | bytes 221192 | tf_op jit(solution)/shard_map/ppermute | solution.py:125
  119.3 11.9 %collective-permute-start.17 = (bf16[48,768]{1,0:T(8,128)(2,1)S(1)}, bf16[48,768]{1,0:T(8,128)(2,1)S(1)}, u32[]{:S(2)}, u32[]{:S(2)}) collective-permute-start(bf16[48,768]{1,0:T(8,128)(2,1)S(1)} %get-tuple-element.43), channel_id=1, source_target_pairs={{0,8},{4,12},{8,0},{12,4},{1,9},{5,13},{9,1},{13,5},{2,10},{6,14},... | collective-permute-start | bytes 221192 | tf_op jit(solution)/shard_map/ppermute | solution.py:125
  120.2 10.9 %collective-permute-start.18 = (bf16[48,768]{1,0:T(8,128)(2,1)S(1)}, bf16[48,768]{1,0:T(8,128)(2,1)S(1)}, u32[]{:S(2)}, u32[]{:S(2)}) collective-permute-start(bf16[48,768]{1,0:T(8,128)(2,1)S(1)} %get-tuple-element.42), channel_id=1, source_target_pairs={{0,4},{4,8},{8,12},{12,0},{1,5},{5,9},{9,13},{13,1},{2,6},{6,10},{... | collective-permute-start | bytes 221192 | tf_op jit(solution)/shard_map/ppermute | solution.py:125
  120.3 10.9 %collective-permute-start.24 = (bf16[48,768]{1,0:T(8,128)(2,1)S(1)}, bf16[48,768]{1,0:T(8,128)(2,1)S(1)}, u32[]{:S(2)}, u32[]{:S(2)}) collective-permute-start(bf16[48,768]{1,0:T(8,128)(2,1)S(1)} %get-tuple-element.48), channel_id=1, source_target_pairs={{0,12},{4,0},{8,4},{12,8},{1,13},{5,1},{9,5},{13,9},{2,14},{6,2},{... | collective-permute-start | bytes 221192 | tf_op jit(solution)/shard_map/ppermute | solution.py:125
  124.2 9.7 %collective-permute-start.25 = (bf16[48,768]{1,0:T(8,128)(2,1)S(1)}, bf16[48,768]{1,0:T(8,128)(2,1)S(1)}, u32[]{:S(2)}, u32[]{:S(2)}) collective-permute-start(bf16[48,768]{1,0:T(8,128)(2,1)S(1)} %get-tuple-element.47), channel_id=1, source_target_pairs={{0,8},{4,12},{8,0},{12,4},{1,9},{5,13},{9,1},{13,5},{2,10},{6,14},... | collective-permute-start | bytes 221192 | tf_op jit(solution)/shard_map/ppermute | solution.py:125
  124.4 9.5 %collective-permute-start.26 = (bf16[48,768]{1,0:T(8,128)(2,1)S(1)}, bf16[48,768]{1,0:T(8,128)(2,1)S(1)}, u32[]{:S(2)}, u32[]{:S(2)}) collective-permute-start(bf16[48,768]{1,0:T(8,128)(2,1)S(1)} %get-tuple-element.46), channel_id=1, source_target_pairs={{0,4},{4,8},{8,12},{12,0},{1,5},{5,9},{9,13},{13,1},{2,6},{6,10},{... | collective-permute-start | bytes 221192 | tf_op jit(solution)/shard_map/ppermute | solution.py:125

commit v3 on v2

--- a/solution.py
+++ b/solution.py
@@ -3,6 +3,8 @@
 import jax
 import jax.numpy as jnp
 from jax import lax
+from jax.experimental import pallas as pl
+from jax.experimental.pallas import tpu as pltpu
 from jax.sharding import PartitionSpec as P
 
 HD = 128
@@ -16,6 +18,199 @@
 epsilon = 1e-05
 highest = lax.Precision.HIGHEST
 floor_score = -1e30
+
+
+MESH = pl.DeviceIdType.MESH
+WIDTH = 512
+LAG = 3
+
+
+def expert_kernel(
+    n, held, pieces, tiles, gate, down, out,
+    rows, gate_buf, down_buf, part, came, acc, swap_out, swap_in, back, landed,
+    gate_sem, down_sem, go_send, go_recv, pass_send, pass_recv, x_send, x_recv,
+    swap_send, swap_recv, back_send, back_recv,
+):
+    me, exp, tp = lax.axis_index("ctx"), lax.axis_index("exp"), lax.axis_index("tp")
+    total = held * pieces
+    count, half = rows.shape[2], rows.shape[3]
+
+    def fetch_gate(k):
+        columns = pl.ds(pl.multiple_of(k * WIDTH, WIDTH), WIDTH)
+        return pltpu.make_async_copy(gate.at[:, columns], gate_buf.at[k % 2], gate_sem.at[k % 2])
+
+    def fetch_down(k):
+        lines = pl.ds(pl.multiple_of(k * WIDTH, WIDTH), WIDTH)
+        return pltpu.make_async_copy(down.at[lines], down_buf.at[k % 2], down_sem.at[k % 2])
+
+    def remote(src, dst, send, recv, where):
+        return pltpu.make_async_remote_copy(
+            src_ref=src, dst_ref=dst, send_sem=send, recv_sem=recv,
+            device_id=where, device_id_type=MESH,
+        )
+
+    def go(e, shift):
+        spot = pl.ds(shift * C, C)
+        return remote(
+            tiles.at[e, spot], rows.at[e, tp, spot], go_send.at[e, shift], go_recv.at[e, shift],
+            {"ctx": lax.rem(me + shift, n)},
+        )
+
+    def hand_over(e):
+        return remote(
+            rows.at[e, tp], rows.at[e, tp], pass_send.at[e], pass_recv.at[e], {"tp": 1 - tp}
+        )
+
+    def cross(k):
+        return remote(part.at[k], came.at[k], x_send.at[k], x_recv.at[k], {"exp": 1 - exp})
+
+    def swap(e):
+        return remote(swap_out.at[e], swap_in.at[e], swap_send.at[e], swap_recv.at[e], {"tp": 1 - tp})
+
+    def give(e, shift):
+        spot = pl.ds(shift * C, C)
+        return remote(
+            back.at[e, spot], landed.at[e, spot], back_send.at[e, shift], back_recv.at[e, shift],
+            {"ctx": lax.rem(me + n - shift, n)},
+        )
+
+    fetch_gate(0).start()
+    fetch_down(0).start()
+    barrier = pltpu.get_barrier_semaphore()
+    for shift in range(1, n):
+        pl.semaphore_signal(
+            barrier, inc=1, device_id={"ctx": lax.rem(me + shift, n)}, device_id_type=MESH
+        )
+    pl.semaphore_signal(barrier, inc=1, device_id={"exp": 1 - exp}, device_id_type=MESH)
+    pl.semaphore_signal(barrier, inc=1, device_id={"tp": 1 - tp}, device_id_type=MESH)
+    pl.semaphore_wait(barrier, n + 1)
+    for e in range(held):
+        for shift in range(1, n):
+            go(e, shift).start()
+    for e in range(held):
+        rows[e, tp, :C] = tiles[e, :C]
+
+    def step(k, carry):
+        @pl.when(k < total)
+        def _():
+            e = k // pieces
+
+            @pl.when(k % pieces == 0)
+            def _():
+                for shift in range(1, n):
+                    go(e, shift).wait_recv()
+                hand_over(e).start()
+                hand_over(e).wait_recv()
+
+            @pl.when(k + 1 < total)
+            def _():
+                fetch_gate(k + 1).start()
+
+            fetch_gate(k).wait()
+            product = jnp.dot(
+                rows[e, 0], gate_buf[k % 2, :half], preferred_element_type=jnp.float32
+            ) + jnp.dot(rows[e, 1], gate_buf[k % 2, half:], preferred_element_type=jnp.float32)
+            part[k] = product.astype(jnp.bfloat16)
+            cross(k).start()
+
+        @pl.when(k >= LAG)
+        def _():
+            j = k - LAG
+            e = j // pieces
+
+            @pl.when(j + 1 < total)
+            def _():
+                fetch_down(j + 1).start()
+
+            cross(j).wait_recv()
+            pre_act = part[j].astype(jnp.float32) + came[j].astype(jnp.float32)
+            hidden = jax.nn.silu(pre_act).astype(jnp.bfloat16)
+            fetch_down(j).wait()
+            product = jnp.dot(hidden, down_buf[j % 2], preferred_element_type=jnp.float32)
+
+            @pl.when(j % pieces == 0)
+            def _():
+                acc[...] = product
+
+            @pl.when(j % pieces != 0)
+            def _():
+                acc[...] += product
+
+            @pl.when(j % pieces == pieces - 1)
+            def _():
+                far = pl.ds(pl.multiple_of((1 - tp) * half, 128), half)
+                near = pl.ds(pl.multiple_of(tp * half, 128), half)
+                swap_out[e] = acc[:, far].astype(jnp.bfloat16)
+                swap(e).start()
+                swap(e).wait_recv()
+                back[e] = (acc[:, near] + swap_in[e].astype(jnp.float32)).astype(jnp.bfloat16)
+                for shift in range(1, n):
+                    give(e, shift).start()
+
+        return carry
+
+    lax.fori_loop(0, total + LAG, step, 0)
+    for e in range(held):
+        out[e, :C] = back[e, :C]
+        for shift in range(1, n):
+            give(e, shift).wait_recv()
+            out[e, shift * C : (shift + 1) * C] = landed[e, shift * C : (shift + 1) * C]
+
+    def drain(k, carry):
+        cross(k).wait_send()
+        return carry
+
+    lax.fori_loop(0, total, drain, 0)
+    for e in range(held):
+        hand_over(e).wait_send()
+        swap(e).wait_send()
+        for shift in range(1, n):
+            go(e, shift).wait_send()
+            give(e, shift).wait_send()
+
+
+def run_experts(tiles, gate, down, n, held):
+    depth, units = gate.shape
+    pieces = units // held // WIDTH
+    total = held * pieces
+    count, half = tiles.shape[1], tiles.shape[2]
+    wide = down.shape[1]
+    dma = pltpu.SemaphoreType.DMA
+    return pl.pallas_call(
+        lambda *refs: expert_kernel(n, held, pieces, *refs),
+        out_shape=jax.ShapeDtypeStruct((held, count, wide // 2), jnp.bfloat16),
+        in_specs=[
+            pl.BlockSpec(memory_space=pltpu.VMEM),
+            pl.BlockSpec(memory_space=pl.ANY),
+            pl.BlockSpec(memory_space=pl.ANY),
+        ],
+        out_specs=pl.BlockSpec(memory_space=pltpu.VMEM),
+        scratch_shapes=[
+            pltpu.VMEM((held, 2, count, half), jnp.bfloat16),
+            pltpu.VMEM((2, depth, WIDTH), jnp.bfloat16),
+            pltpu.VMEM((2, WIDTH, wide), jnp.bfloat16),
+            pltpu.VMEM((total, count, WIDTH), jnp.bfloat16),
+            pltpu.VMEM((total, count, WIDTH), jnp.bfloat16),
+            pltpu.VMEM((count, wide), jnp.float32),
+            pltpu.VMEM((held, count, wide // 2), jnp.bfloat16),
+            pltpu.VMEM((held, count, wide // 2), jnp.bfloat16),
+            pltpu.VMEM((held, count, wide // 2), jnp.bfloat16),
+            pltpu.VMEM((held, count, wide // 2), jnp.bfloat16),
+            dma((2,)), dma((2,)),
+            dma((held, n)), dma((held, n)),
+            dma((held,)), dma((held,)),
+            dma((total,)), dma((total,)),
+            dma((held,)), dma((held,)),
+            dma((held, n)), dma((held, n)),
+        ],
+        compiler_params=pltpu.CompilerParams(
+            collective_id=0, has_side_effects=True, vmem_limit_bytes=48 * 2**20
+        ),
+        cost_estimate=pl.CostEstimate(
+            flops=4 * held * count * depth * units // held, bytes_accessed=4 * depth * units,
+            transcendentals=0,
+        ),
+    )(tiles, gate, down)
 
 
 def per_device(
@@ -116,6 +311,21 @@
     )
     send_tiles = send_tiles.reshape(experts_held, E // experts_held, C, -1)
 
+    if direct and exp_count == 2 and gate_weight.shape[2] // experts_held % WIDTH == 0:
+        returned = run_experts(
+            send_tiles.reshape(experts_held, ctx_count * C, -1),
+            gate_weight.reshape(gate_weight.shape[0], -1),
+            down_weight.reshape(-1, down_weight.shape[2]),
+            ctx_count,
+            experts_held,
+        )
+        moe_mine = jnp.dot(
+            combine_matrix,
+            returned.reshape(E * C, -1).astype(jnp.float32),
+            precision=highest,
+        )
+        return (mixed_in + moe_mine).astype(jnp.bfloat16)
+
     def exchange(tiles, sign):
         if not direct:
             return lax.all_to_all(tiles, "ctx", split_axis=0, concat_axis=0, tiled=True)

time: 136 us -> 119 us (0.88)
  Pallas kernels: 0 us -> 94.8 us
  waiting for transfers between devices: 50.8 us -> 3.2 us
  starting transfers between devices: 41.7 us -> 12.2 us
  matrix products: 31.9 us -> 2.76 us
  blocking collectives: 4.62 us -> 0 us
    pallas_call x0 -> x1, Pallas kernels: none -> 94.8 us  [run_experts(): pl.pallas_call(lambda *refs: expert_kernel(n, held, pieces, *refs), out_s...]
    ppermute x22 -> x0, waiting for transfers between devices: 47.6 us -> none  [the longest x8 39.2 us: per_device(): others.append(lax.ppermute(part, 'exp', turned))]
    ppermute x22 -> x0, starting transfers between devices: 29.4 us -> none  [the longest x12 19.8 us: exchange(): moved.append(lax.ppermute(tiles[shift], 'ctx', turned))]
    dot_general x18 -> x1, matrix products: 30.3 us -> 1.15 us  [per_device(): jnp.dot(combine_matrix, returned.reshape(E * C, -1).astype(jnp.float32),...]
    all_gather x2 -> x0, blocking collectives: 4.62 us -> none  [per_device(): arrived = lax.all_gather(half, 'tp', axis=1, tiled=True)]
  transfers between devices with their start and end apart: 27 -> 5, of which waited for: 14 -> 2; matrix products, arithmetic and copies ran while one was open for 25% -> 3% of each run, Pallas kernels for 0% -> 0%
where the time goes in v3:
time: 119 us
  Pallas kernels  94.8 us (80%)
  starting transfers between devices  12.2 us (10%)
  local copies, waits for them, and re-layouts  3.85 us (3%)
  waiting for transfers between devices  3.2 us (3%)
  matrix products  2.76 us (2%)
  other arithmetic  1.68 us (1%)
    pallas_call x1, Pallas kernels, run_experts(): pl.pallas_call(lambda *refs: expert_kernel(n, held, pieces, *refs), out_s...  94.8 us
    ppermute x3, starting transfers between devices, per_device(): pieces_kv.append(lax.ppermute(pair, 'ctx', later))  10.7 us
    ppermute x2, waiting for transfers between devices, per_device(): lax.ppermute(stats, ('exp', 'tp'), [(j, j ^ flip) for j in range(ways)])  3.18 us
  transfers between devices with their start and end apart: 5, of which 2 were waited for; matrix products, arithmetic and copies ran while one was open for 3% of the time, Pallas kernels for 0%

profile of v3, /device:TPU:0, one launch (start us, length us, event | category | flops | bytes accessed | tf_op | source)
XLA Modules:
  0.0 118.8 jit_solution(15785296033352468350)
XLA Ops:
  0.0 0.0 copy-start
  0.0 0.8 constant_dynamic-slice_fusion
  0.8 4.9 %collective-permute-start = (bf16[128,256]{1,0:T(8,128)(2,1)S(1)}, bf16[128,256]{1,0:T(8,128)(2,1)S(1)}, u32[]{:S(2)}, u32[]{:S(2)}) collective-permute-start(bf16[128,256]{1,0:T(8,128)(2,1)S(1)} %pad_maximum_fusion.1), channel_id=1, source_target_pairs={{0,4},{4,8},{8,12},{1,5},{5,9},{9,13},{2,6},{6,10},{10,14},{3,7},{... | collective-permute-start | bytes 196616 | tf_op jit(solution)/shard_map/ppermute | solution.py:250
  5.7 4.5 %collective-permute-start.1 = (bf16[128,256]{1,0:T(8,128)(2,1)S(1)}, bf16[128,256]{1,0:T(8,128)(2,1)S(1)}, u32[]{:S(2)}, u32[]{:S(2)}) collective-permute-start(bf16[128,256]{1,0:T(8,128)(2,1)S(1)} %pad_maximum_fusion.1), channel_id=1, source_target_pairs={{0,8},{4,12},{1,9},{5,13},{2,10},{6,14},{3,11},{7,15},{16,24},{20,... | collective-permute-start | bytes 196616 | tf_op jit(solution)/shard_map/ppermute | solution.py:250
  10.2 1.3 %collective-permute-start.2 = (bf16[128,256]{1,0:T(8,128)(2,1)S(1)}, bf16[128,256]{1,0:T(8,128)(2,1)S(1)}, u32[]{:S(2)}, u32[]{:S(2)}) collective-permute-start(bf16[128,256]{1,0:T(8,128)(2,1)S(1)} %pad_maximum_fusion.1), channel_id=1, source_target_pairs={{0,12},{1,13},{2,14},{3,15},{16,28},{17,29},{18,30},{19,31}} | collective-permute-start | bytes 196616 | tf_op jit(solution)/shard_map/ppermute | solution.py:250
  11.6 0.8 copy.70
  12.4 0.1 eq.58
  12.5 0.1 eq.54
  12.7 1.1 copy.65
  13.8 0.6 reduce-window.6
  14.4 0.2 slice_reduce_fusion
  14.6 0.2 compare_and_fusion
  14.8 0.1 fusion.13
  14.9 0.1 reduce_sum.49
  15.1 0.1 copy.72
  15.1 0.0 collective-permute-done
  15.1 0.0 collective-permute-done.1
  15.1 0.0 collective-permute-done.2
  15.2 0.4 fusion.28
  15.6 0.2 fusion
  15.8 0.0 copy-start.1
  15.8 0.0 copy-start.2
  15.8 0.4 fusion.2
  16.2 0.0 copy-start.3
  16.2 0.2 copy.69
  16.4 0.3 copy-done.1
  16.7 0.1 multiply_reduce_fusion
  16.9 0.0 copy-done
  16.9 0.0 copy-done.2
  16.9 0.4 fusion.7
  17.3 0.0 collective-permute-start.3
  17.4 0.0 copy-done.3
  17.4 1.1 collective-permute-done.3
  18.5 1.5 %collective-permute-start.4 = (f32[9,128]{1,0:T(8,128)S(1)}, f32[9,128]{1,0:T(8,128)S(1)}, u32[]{:S(2)}, u32[]{:S(2)}) collective-permute-start(f32[9,128]{1,0:T(8,128)S(1)} %fusion.27), channel_id=1, source_target_pairs={{0,2},{1,3},{2,0},{3,1},{4,6},{5,7},{6,4},{7,5},{8,10},{9,11},{10,... | collective-permute-start | bytes 13832 | tf_op jit(solution)/shard_map/ppermute | solution.py:280
  20.0 0.1 fusion.6
  20.1 2.1 %collective-permute-done.4 = f32[9,128]{1,0:T(8,128)S(1)} collective-permute-done((f32[9,128]{1,0:T(8,128)S(1)}, f32[9,128]{1,0:T(8,128)S(1)}, u32[]{:S(2)}, u32[]{:S(2)}) %collective-permute-start.4) | collective-permute-done | bytes 4640 | tf_op jit(solution)/shard_map/ppermute | solution.py:280
  22.2 0.4 convolution_convert_fusion
  22.7 0.1 select_reduce_fusion
  22.8 94.8 %shard_map.91 = bf16[2,192,768]{2,1,0:T(8,128)(2,1)S(1)} custom-call(bf16[2,192,768]{2,1,0:T(8,128)(2,1)S(1)} %bitcast.44, bf16[1536,8192]{1,0:T(8,128)(2,1)} %bitcast.45, bf16[8192,1536]{1,0:T(8,128)(2,1)} %bitcast.46), custom_call_target="tpu_custom_call" | custom-call | flops 9663676416 | bytes 50331648 | tf_op jit(solution)/shard_map/pallas_call | solution.py:179
  117.6 1.1 fusion.3
  (17 shorter events, 0.2 us)
Async XLA Ops:
  0.0 16.9 %copy-start = (f32[768,8]{0,1:T(8,128)S(1)}, f32[768,8]{0,1:T(8,128)}, u32[]{:S(2)}) copy-start(f32[768,8]{0,1:T(8,128)} %param.14) | copy-start | bytes 73732
  0.8 14.3 %collective-permute-start = (bf16[128,256]{1,0:T(8,128)(2,1)S(1)}, bf16[128,256]{1,0:T(8,128)(2,1)S(1)}, u32[]{:S(2)}, u32[]{:S(2)}) collective-permute-start(bf16[128,256]{1,0:T(8,128)(2,1)S(1)} %pad_maximum_fusion.1), channel_id=1, source_target_pairs={{0,4},{4,8},{8,12},{1,5},{5,9},{9,13},{2,6},{6,10},{10,14},{3,7},{... | collective-permute-start | bytes 196616 | tf_op jit(solution)/shard_map/ppermute | solution.py:250
  5.7 9.4 %collective-permute-start.1 = (bf16[128,256]{1,0:T(8,128)(2,1)S(1)}, bf16[128,256]{1,0:T(8,128)(2,1)S(1)}, u32[]{:S(2)}, u32[]{:S(2)}) collective-permute-start(bf16[128,256]{1,0:T(8,128)(2,1)S(1)} %pad_maximum_fusion.1), channel_id=1, source_target_pairs={{0,8},{4,12},{1,9},{5,13},{2,10},{6,14},{3,11},{7,15},{16,24},{20,... | collective-permute-start | bytes 196616 | tf_op jit(solution)/shard_map/ppermute | solution.py:250
  10.2 4.9 %collective-permute-start.2 = (bf16[128,256]{1,0:T(8,128)(2,1)S(1)}, bf16[128,256]{1,0:T(8,128)(2,1)S(1)}, u32[]{:S(2)}, u32[]{:S(2)}) collective-permute-start(bf16[128,256]{1,0:T(8,128)(2,1)S(1)} %pad_maximum_fusion.1), channel_id=1, source_target_pairs={{0,12},{1,13},{2,14},{3,15},{16,28},{17,29},{18,30},{19,31}} | collective-permute-start | bytes 196616 | tf_op jit(solution)/shard_map/ppermute | solution.py:250
  15.8 0.9 copy-start.1
  15.8 1.1 copy-start.2
  16.2 1.1 copy-start.3
  17.3 1.2 %collective-permute-start.3 = (f32[9,128]{1,0:T(8,128)S(1)}, f32[9,128]{1,0:T(8,128)S(1)}, u32[]{:S(2)}, u32[]{:S(2)}) collective-permute-start(f32[9,128]{1,0:T(8,128)S(1)} %maximum_bitcast_fusion), channel_id=1, source_target_pairs={{0,1},{1,0},{2,3},{3,2},{4,5},{5,4},{6,7},{7,6},{8,9},{9,8},{10,11... | collective-permute-start | bytes 13832 | tf_op jit(solution)/shard_map/ppermute | solution.py:280
  18.5 3.7 %collective-permute-start.4 = (f32[9,128]{1,0:T(8,128)S(1)}, f32[9,128]{1,0:T(8,128)S(1)}, u32[]{:S(2)}, u32[]{:S(2)}) collective-permute-start(f32[9,128]{1,0:T(8,128)S(1)} %fusion.27), channel_id=1, source_target_pairs={{0,2},{1,3},{2,0},{3,1},{4,6},{5,7},{6,4},{7,5},{8,10},{9,11},{10,... | collective-permute-start | bytes 13832 | tf_op jit(solution)/shard_map/ppermute | solution.py:280

commit v4 on v3

--- a/solution.py
+++ b/solution.py
@@ -21,7 +21,7 @@
 
 
 MESH = pl.DeviceIdType.MESH
-WIDTH = 512
+WIDTH = 1024
 LAG = 3
 
 
@@ -32,16 +32,28 @@
     swap_send, swap_recv, back_send, back_recv,
 ):
     me, exp, tp = lax.axis_index("ctx"), lax.axis_index("exp"), lax.axis_index("tp")
-    total = held * pieces
-    count, half = rows.shape[2], rows.shape[3]
+    units = 2 * held
+    per = n // 2
+    total = units * pieces
+    half = rows.shape[3]
+
+    def shift_of(u, p):
+        spot = (u % 2) * per + p
+        return (spot + per) % n if u // 2 == held - 1 else spot
+
+    every = [(u, p) for u in range(units) for p in range(per)]
+    away = [(u, p) for u, p in every if shift_of(u, p)]
+    here = [(u, p) for u, p in every if not shift_of(u, p)]
+
+    def block_of(k):
+        place = (k // pieces // 2) * pieces + k % pieces
+        return pl.ds(pl.multiple_of(place * WIDTH, WIDTH), WIDTH)
 
     def fetch_gate(k):
-        columns = pl.ds(pl.multiple_of(k * WIDTH, WIDTH), WIDTH)
-        return pltpu.make_async_copy(gate.at[:, columns], gate_buf.at[k % 2], gate_sem.at[k % 2])
+        return pltpu.make_async_copy(gate.at[:, block_of(k)], gate_buf.at[k % 2], gate_sem.at[k % 2])
 
     def fetch_down(k):
-        lines = pl.ds(pl.multiple_of(k * WIDTH, WIDTH), WIDTH)
-        return pltpu.make_async_copy(down.at[lines], down_buf.at[k % 2], down_sem.at[k % 2])
+        return pltpu.make_async_copy(down.at[block_of(k)], down_buf.at[k % 2], down_sem.at[k % 2])
 
     def remote(src, dst, send, recv, where):
         return pltpu.make_async_remote_copy(
@@ -49,11 +61,11 @@
             device_id=where, device_id_type=MESH,
         )
 
-    def go(e, shift):
-        spot = pl.ds(shift * C, C)
+    def go(u, p):
+        spot = pl.ds(p * C, C)
         return remote(
-            tiles.at[e, spot], rows.at[e, tp, spot], go_send.at[e, shift], go_recv.at[e, shift],
-            {"ctx": lax.rem(me + shift, n)},
+            tiles.at[u, spot], rows.at[u, tp, spot], go_send.at[u, p], go_recv.at[u, p],
+            {"ctx": lax.rem(me + shift_of(u, p), n)},
         )
 
     def hand_over(e):
@@ -67,11 +79,11 @@
     def swap(e):
         return remote(swap_out.at[e], swap_in.at[e], swap_send.at[e], swap_recv.at[e], {"tp": 1 - tp})
 
-    def give(e, shift):
-        spot = pl.ds(shift * C, C)
+    def give(u, p):
+        spot = pl.ds(p * C, C)
         return remote(
-            back.at[e, spot], landed.at[e, spot], back_send.at[e, shift], back_recv.at[e, shift],
-            {"ctx": lax.rem(me + n - shift, n)},
+            back.at[u, spot], landed.at[u, spot], back_send.at[u, p], back_recv.at[u, p],
+            {"ctx": lax.rem(me + n - shift_of(u, p), n)},
         )
 
     fetch_gate(0).start()
@@ -84,23 +96,39 @@
     pl.semaphore_signal(barrier, inc=1, device_id={"exp": 1 - exp}, device_id_type=MESH)
     pl.semaphore_signal(barrier, inc=1, device_id={"tp": 1 - tp}, device_id_type=MESH)
     pl.semaphore_wait(barrier, n + 1)
-    for e in range(held):
-        for shift in range(1, n):
-            go(e, shift).start()
-    for e in range(held):
-        rows[e, tp, :C] = tiles[e, :C]
+    for u, p in away:
+        if u == 0:
+            go(u, p).start()
+    for u, p in here:
+        rows[u, tp, p * C : (p + 1) * C] = tiles[u, p * C : (p + 1) * C]
+
+    def receive(u):
+        for v, p in away:
+            if v == u:
+                go(v, p).wait_recv()
+        hand_over(u).start()
+        for v, p in away:
+            if v == u + 1:
+                go(v, p).start()
+        hand_over(u).wait_recv()
+
+    def finish(u):
+        far = pl.ds(pl.multiple_of((1 - tp) * half, 128), half)
+        near = pl.ds(pl.multiple_of(tp * half, 128), half)
+        swap_out[u] = acc[:, far].astype(jnp.bfloat16)
+        swap(u).start()
+        swap(u).wait_recv()
+        back[u] = (acc[:, near] + swap_in[u].astype(jnp.float32)).astype(jnp.bfloat16)
+        for v, p in away:
+            if v == u:
+                give(v, p).start()
 
     def step(k, carry):
         @pl.when(k < total)
         def _():
             e = k // pieces
-
-            @pl.when(k % pieces == 0)
-            def _():
-                for shift in range(1, n):
-                    go(e, shift).wait_recv()
-                hand_over(e).start()
-                hand_over(e).wait_recv()
+            for u in range(units):
+                pl.when(k == u * pieces)(lambda u=u: receive(u))
 
             @pl.when(k + 1 < total)
             def _():
@@ -136,49 +164,42 @@
             def _():
                 acc[...] += product
 
-            @pl.when(j % pieces == pieces - 1)
-            def _():
-                far = pl.ds(pl.multiple_of((1 - tp) * half, 128), half)
-                near = pl.ds(pl.multiple_of(tp * half, 128), half)
-                swap_out[e] = acc[:, far].astype(jnp.bfloat16)
-                swap(e).start()
-                swap(e).wait_recv()
-                back[e] = (acc[:, near] + swap_in[e].astype(jnp.float32)).astype(jnp.bfloat16)
-                for shift in range(1, n):
-                    give(e, shift).start()
+            for u in range(units):
+                pl.when(j == (u + 1) * pieces - 1)(lambda u=u: finish(u))
 
         return carry
 
     lax.fori_loop(0, total + LAG, step, 0)
-    for e in range(held):
-        out[e, :C] = back[e, :C]
-        for shift in range(1, n):
-            give(e, shift).wait_recv()
-            out[e, shift * C : (shift + 1) * C] = landed[e, shift * C : (shift + 1) * C]
+    for u, p in here:
+        out[u, p * C : (p + 1) * C] = back[u, p * C : (p + 1) * C]
+    for u, p in away:
+        give(u, p).wait_recv()
+        out[u, p * C : (p + 1) * C] = landed[u, p * C : (p + 1) * C]
 
     def drain(k, carry):
         cross(k).wait_send()
         return carry
 
     lax.fori_loop(0, total, drain, 0)
-    for e in range(held):
-        hand_over(e).wait_send()
-        swap(e).wait_send()
-        for shift in range(1, n):
-            go(e, shift).wait_send()
-            give(e, shift).wait_send()
+    for u in range(units):
+        hand_over(u).wait_send()
+        swap(u).wait_send()
+    for u, p in away:
+        go(u, p).wait_send()
+        give(u, p).wait_send()
 
 
 def run_experts(tiles, gate, down, n, held):
     depth, units = gate.shape
     pieces = units // held // WIDTH
-    total = held * pieces
+    parts = 2 * held
+    total = parts * pieces
     count, half = tiles.shape[1], tiles.shape[2]
     wide = down.shape[1]
     dma = pltpu.SemaphoreType.DMA
     return pl.pallas_call(
         lambda *refs: expert_kernel(n, held, pieces, *refs),
-        out_shape=jax.ShapeDtypeStruct((held, count, wide // 2), jnp.bfloat16),
+        out_shape=jax.ShapeDtypeStruct((parts, count, wide // 2), jnp.bfloat16),
         in_specs=[
             pl.BlockSpec(memory_space=pltpu.VMEM),
             pl.BlockSpec(memory_space=pl.ANY),
@@ -186,28 +207,28 @@
         ],
         out_specs=pl.BlockSpec(memory_space=pltpu.VMEM),
         scratch_shapes=[
-            pltpu.VMEM((held, 2, count, half), jnp.bfloat16),
+            pltpu.VMEM((parts, 2, count, half), jnp.bfloat16),
             pltpu.VMEM((2, depth, WIDTH), jnp.bfloat16),
             pltpu.VMEM((2, WIDTH, wide), jnp.bfloat16),
             pltpu.VMEM((total, count, WIDTH), jnp.bfloat16),
             pltpu.VMEM((total, count, WIDTH), jnp.bfloat16),
             pltpu.VMEM((count, wide), jnp.float32),
-            pltpu.VMEM((held, count, wide // 2), jnp.bfloat16),
-            pltpu.VMEM((held, count, wide // 2), jnp.bfloat16),
-            pltpu.VMEM((held, count, wide // 2), jnp.bfloat16),
-            pltpu.VMEM((held, count, wide // 2), jnp.bfloat16),
+            pltpu.VMEM((parts, count, wide // 2), jnp.bfloat16),
+            pltpu.VMEM((parts, count, wide // 2), jnp.bfloat16),
+            pltpu.VMEM((parts, count, wide // 2), jnp.bfloat16),
+            pltpu.VMEM((parts, count, wide // 2), jnp.bfloat16),
             dma((2,)), dma((2,)),
-            dma((held, n)), dma((held, n)),
-            dma((held,)), dma((held,)),
+            dma((parts, n // 2)), dma((parts, n // 2)),
+            dma((parts,)), dma((parts,)),
             dma((total,)), dma((total,)),
-            dma((held,)), dma((held,)),
-            dma((held, n)), dma((held, n)),
+            dma((parts,)), dma((parts,)),
+            dma((parts, n // 2)), dma((parts, n // 2)),
         ],
         compiler_params=pltpu.CompilerParams(
             collective_id=0, has_side_effects=True, vmem_limit_bytes=48 * 2**20
         ),
         cost_estimate=pl.CostEstimate(
-            flops=4 * held * count * depth * units // held, bytes_accessed=4 * depth * units,
+            flops=8 * held * count * depth * units // held, bytes_accessed=8 * depth * units,
             transcendentals=0,
         ),
     )(tiles, gate, down)
@@ -296,9 +317,18 @@
     slot_index = jnp.sum((jnp.cumsum(flat_hot, axis=0) - flat_hot) * flat_hot, axis=1)
     ctx_sharing = max(1, ctx_count // E)
     experts_held = max(1, E // ctx_count)
+    kernel_path = (
+        direct
+        and exp_count == 2
+        and ctx_count % 2 == 0
+        and gate_weight.shape[2] // experts_held % WIDTH == 0
+    )
     if direct:
         away = (flat_ids // experts_held - lax.axis_index("ctx") + ctx_count) % ctx_count
-        tile_index = (flat_ids % experts_held) * ctx_count + away
+        local = flat_ids % experts_held
+        if kernel_path:
+            away = (away + (local == experts_held - 1) * (ctx_count // 2)) % ctx_count
+        tile_index = local * ctx_count + away
     else:
         tile_index = (flat_ids % experts_held) * (E // experts_held) + flat_ids // experts_held
     tile_row = (tile_index * C + slot_index).reshape(row_count, 2)
@@ -311,9 +341,9 @@
     )
     send_tiles = send_tiles.reshape(experts_held, E // experts_held, C, -1)
 
-    if direct and exp_count == 2 and gate_weight.shape[2] // experts_held % WIDTH == 0:
+    if kernel_path:
         returned = run_experts(
-            send_tiles.reshape(experts_held, ctx_count * C, -1),
+            send_tiles.reshape(2 * experts_held, ctx_count // 2 * C, -1),
             gate_weight.reshape(gate_weight.shape[0], -1),
             down_weight.reshape(-1, down_weight.shape[2]),
             ctx_count,

time: 119 us -> 107 us (0.90)
  Pallas kernels: 94.8 us -> 82.8 us
    pallas_call x1, Pallas kernels: 94.8 us -> 82.8 us  [run_experts(): pl.pallas_call(lambda *refs: expert_kernel(n, held, pieces, *refs), out_s...]
where the time goes in v4:
time: 107 us
  Pallas kernels  82.8 us (77%)
  starting transfers between devices  12.2 us (11%)
  local copies, waits for them, and re-layouts  3.85 us (4%)
  waiting for transfers between devices  3.19 us (3%)
  matrix products  2.75 us (3%)
  other arithmetic  1.69 us (2%)
    pallas_call x1, Pallas kernels, run_experts(): pl.pallas_call(lambda *refs: expert_kernel(n, held, pieces, *refs), out_s...  82.8 us
    ppermute x3, starting transfers between devices, per_device(): pieces_kv.append(lax.ppermute(pair, 'ctx', later))  10.7 us
    ppermute x2, waiting for transfers between devices, per_device(): lax.ppermute(stats, ('exp', 'tp'), [(j, j ^ flip) for j in range(ways)])  3.17 us
    unnamed x10, local copies, waits for them, and re-layouts  2.22 us
  transfers between devices with their start and end apart: 5, of which 2 were waited for; matrix products, arithmetic and copies ran while one was open for 3% of the time, Pallas kernels for 0%

profile of v4, /device:TPU:0, one launch (start us, length us, event | category | flops | bytes accessed | tf_op | source)
XLA Modules:
  0.0 106.8 jit_solution(14693099210453074280)
XLA Ops:
  0.0 0.0 copy-start
  0.0 0.8 constant_dynamic-slice_fusion
  0.8 4.9 %collective-permute-start = (bf16[128,256]{1,0:T(8,128)(2,1)S(1)}, bf16[128,256]{1,0:T(8,128)(2,1)S(1)}, u32[]{:S(2)}, u32[]{:S(2)}) collective-permute-start(bf16[128,256]{1,0:T(8,128)(2,1)S(1)} %pad_maximum_fusion.1), channel_id=1, source_target_pairs={{0,4},{4,8},{8,12},{1,5},{5,9},{9,13},{2,6},{6,10},{10,14},{3,7},{... | collective-permute-start | bytes 196616 | tf_op jit(solution)/shard_map/ppermute | solution.py:271
  5.7 4.5 %collective-permute-start.1 = (bf16[128,256]{1,0:T(8,128)(2,1)S(1)}, bf16[128,256]{1,0:T(8,128)(2,1)S(1)}, u32[]{:S(2)}, u32[]{:S(2)}) collective-permute-start(bf16[128,256]{1,0:T(8,128)(2,1)S(1)} %pad_maximum_fusion.1), channel_id=1, source_target_pairs={{0,8},{4,12},{1,9},{5,13},{2,10},{6,14},{3,11},{7,15},{16,24},{20,... | collective-permute-start | bytes 196616 | tf_op jit(solution)/shard_map/ppermute | solution.py:271
  10.2 1.3 %collective-permute-start.2 = (bf16[128,256]{1,0:T(8,128)(2,1)S(1)}, bf16[128,256]{1,0:T(8,128)(2,1)S(1)}, u32[]{:S(2)}, u32[]{:S(2)}) collective-permute-start(bf16[128,256]{1,0:T(8,128)(2,1)S(1)} %pad_maximum_fusion.1), channel_id=1, source_target_pairs={{0,12},{1,13},{2,14},{3,15},{16,28},{17,29},{18,30},{19,31}} | collective-permute-start | bytes 196616 | tf_op jit(solution)/shard_map/ppermute | solution.py:271
  11.6 0.8 copy.70
  12.4 0.1 eq.66
  12.5 0.1 eq.62
  12.7 1.1 %copy.65 = bf16[128,768]{0,1:T(8,128)(2,1)S(1)} copy(bf16[128,768]{1,0:T(8,128)(2,1)} %param.9) | data formatting | bytes 393216 | tf_op args[0]
  13.8 0.6 reduce-window.6
  14.4 0.2 slice_reduce_fusion
  14.6 0.2 compare_and_fusion
  14.8 0.1 fusion.13
  14.9 0.1 reduce_sum.49
  15.1 0.1 copy.72
  15.1 0.0 collective-permute-done
  15.1 0.0 collective-permute-done.1
  15.1 0.0 collective-permute-done.2
  15.2 0.4 fusion.29
  15.6 0.2 fusion
  15.8 0.0 copy-start.1
  15.8 0.0 copy-start.2
  15.8 0.4 fusion.2
  16.2 0.0 copy-start.3
  16.2 0.2 copy.69
  16.4 0.3 copy-done.1
  16.7 0.1 multiply_reduce_fusion
  16.9 0.0 copy-done
  16.9 0.0 copy-done.2
  16.9 0.4 fusion.7
  17.3 0.0 collective-permute-start.3
  17.4 0.0 copy-done.3
  17.4 1.1 %collective-permute-done.3 = f32[9,128]{1,0:T(8,128)S(1)} collective-permute-done((f32[9,128]{1,0:T(8,128)S(1)}, f32[9,128]{1,0:T(8,128)S(1)}, u32[]{:S(2)}, u32[]{:S(2)}) %collective-permute-start.3) | collective-permute-done | bytes 4640 | tf_op jit(solution)/shard_map/ppermute | solution.py:301
  18.5 1.5 %collective-permute-start.4 = (f32[9,128]{1,0:T(8,128)S(1)}, f32[9,128]{1,0:T(8,128)S(1)}, u32[]{:S(2)}, u32[]{:S(2)}) collective-permute-start(f32[9,128]{1,0:T(8,128)S(1)} %fusion.28), channel_id=1, source_target_pairs={{0,2},{1,3},{2,0},{3,1},{4,6},{5,7},{6,4},{7,5},{8,10},{9,11},{10,... | collective-permute-start | bytes 13832 | tf_op jit(solution)/shard_map/ppermute | solution.py:301
  20.0 0.1 fusion.6
  20.1 2.1 %collective-permute-done.4 = f32[9,128]{1,0:T(8,128)S(1)} collective-permute-done((f32[9,128]{1,0:T(8,128)S(1)}, f32[9,128]{1,0:T(8,128)S(1)}, u32[]{:S(2)}, u32[]{:S(2)}) %collective-permute-start.4) | collective-permute-done | bytes 4640 | tf_op jit(solution)/shard_map/ppermute | solution.py:301
  22.2 0.4 convolution_convert_fusion
  22.7 0.1 select_reduce_fusion
  22.8 82.8 %shard_map.91 = bf16[4,96,768]{2,1,0:T(8,128)(2,1)S(1)} custom-call(bf16[4,96,768]{2,1,0:T(8,128)(2,1)S(1)} %bitcast.44, bf16[1536,8192]{1,0:T(8,128)(2,1)} %bitcast.45, bf16[8192,1536]{1,0:T(8,128)(2,1)} %bitcast.46), custom_call_target="tpu_custom_call" | custom-call | flops 9663676416 | bytes 100663296 | tf_op jit(solution)/shard_map/pallas_call | solution.py:200
  105.6 1.1 %fusion.3 = bf16[128,768]{1,0:T(8,128)(2,1)} fusion(f32[128,384]{1,0:T(8,128)S(1)} %select_reduce_fusion, bf16[384,768]{1,0:T(8,128)(2,1)S(1)} %bitcast.43, f32[128,768]{1,0:T(8,128)S(1)} %copy.69, bf16[128,768]{1,0:T(8,128)(2,1)S(1)} %copy-done.1), kind=kOutput, calls=%fused_computation.8 | convolution fusion | flops 453378048 | bytes 1572864 | tf_op jit(solution)/shard_map/dot_general | solution.py:352
  (17 shorter events, 0.2 us)
Async XLA Ops:
  0.0 16.9 %copy-start = (f32[768,8]{0,1:T(8,128)S(1)}, f32[768,8]{0,1:T(8,128)}, u32[]{:S(2)}) copy-start(f32[768,8]{0,1:T(8,128)} %param.14) | copy-start | bytes 73732
  0.8 14.3 %collective-permute-start = (bf16[128,256]{1,0:T(8,128)(2,1)S(1)}, bf16[128,256]{1,0:T(8,128)(2,1)S(1)}, u32[]{:S(2)}, u32[]{:S(2)}) collective-permute-start(bf16[128,256]{1,0:T(8,128)(2,1)S(1)} %pad_maximum_fusion.1), channel_id=1, source_target_pairs={{0,4},{4,8},{8,12},{1,5},{5,9},{9,13},{2,6},{6,10},{10,14},{3,7},{... | collective-permute-start | bytes 196616 | tf_op jit(solution)/shard_map/ppermute | solution.py:271
  5.7 9.4 %collective-permute-start.1 = (bf16[128,256]{1,0:T(8,128)(2,1)S(1)}, bf16[128,256]{1,0:T(8,128)(2,1)S(1)}, u32[]{:S(2)}, u32[]{:S(2)}) collective-permute-start(bf16[128,256]{1,0:T(8,128)(2,1)S(1)} %pad_maximum_fusion.1), channel_id=1, source_target_pairs={{0,8},{4,12},{1,9},{5,13},{2,10},{6,14},{3,11},{7,15},{16,24},{20,... | collective-permute-start | bytes 196616 | tf_op jit(solution)/shard_map/ppermute | solution.py:271
  10.2 4.9 %collective-permute-start.2 = (bf16[128,256]{1,0:T(8,128)(2,1)S(1)}, bf16[128,256]{1,0:T(8,128)(2,1)S(1)}, u32[]{:S(2)}, u32[]{:S(2)}) collective-permute-start(bf16[128,256]{1,0:T(8,128)(2,1)S(1)} %pad_maximum_fusion.1), channel_id=1, source_target_pairs={{0,12},{1,13},{2,14},{3,15},{16,28},{17,29},{18,30},{19,31}} | collective-permute-start | bytes 196616 | tf_op jit(solution)/shard_map/ppermute | solution.py:271
  15.8 0.9 copy-start.1
  15.8 1.1 copy-start.2
  16.2 1.1 %copy-start.3 = (s32[128,2]{0,1:T(2,128)S(1)}, s32[128,2]{0,1:T(2,128)}, u32[]{:S(2)}) copy-start(s32[128,2]{0,1:T(2,128)} %param.15) | copy-start | bytes 3076
  17.3 1.2 %collective-permute-start.3 = (f32[9,128]{1,0:T(8,128)S(1)}, f32[9,128]{1,0:T(8,128)S(1)}, u32[]{:S(2)}, u32[]{:S(2)}) collective-permute-start(f32[9,128]{1,0:T(8,128)S(1)} %maximum_bitcast_fusion), channel_id=1, source_target_pairs={{0,1},{1,0},{2,3},{3,2},{4,5},{5,4},{6,7},{7,6},{8,9},{9,8},{10,11... | collective-permute-start | bytes 13832 | tf_op jit(solution)/shard_map/ppermute | solution.py:301
  18.5 3.7 %collective-permute-start.4 = (f32[9,128]{1,0:T(8,128)S(1)}, f32[9,128]{1,0:T(8,128)S(1)}, u32[]{:S(2)}, u32[]{:S(2)}) collective-permute-start(f32[9,128]{1,0:T(8,128)S(1)} %fusion.28), channel_id=1, source_target_pairs={{0,2},{1,3},{2,0},{3,1},{4,6},{5,7},{6,4},{7,5},{8,10},{9,11},{10,... | collective-permute-start | bytes 13832 | tf_op jit(solution)/shard_map/ppermute | solution.py:301

commit v5 on v4

--- a/solution.py
+++ b/solution.py
@@ -234,6 +234,47 @@
     )(tiles, gate, down)
 
 
+def gather_kernel(n, pair, out, send_sem, recv_sem):
+    me = lax.axis_index("ctx")
+    count = pair.shape[0]
+
+    def hop(shift):
+        return pltpu.make_async_remote_copy(
+            src_ref=pair, dst_ref=out.at[pl.ds(shift * count, count)],
+            send_sem=send_sem.at[shift], recv_sem=recv_sem.at[shift],
+            device_id={"ctx": lax.rem(me + shift, n)}, device_id_type=MESH,
+        )
+
+    barrier = pltpu.get_barrier_semaphore()
+    for shift in range(1, n):
+        pl.semaphore_signal(
+            barrier, inc=1, device_id={"ctx": lax.rem(me + shift, n)}, device_id_type=MESH
+        )
+    pl.semaphore_wait(barrier, n - 1)
+    for shift in range(1, n):
+        pl.when(me + shift < n)(lambda shift=shift: hop(shift).start())
+    out[:count] = pair[...]
+
+    def blank(shift):
+        out[shift * count : (shift + 1) * count] = jnp.zeros(pair.shape, pair.dtype)
+
+    for shift in range(1, n):
+        pl.when(me < shift)(lambda shift=shift: blank(shift))
+        pl.when(me >= shift)(lambda shift=shift: hop(shift).wait_recv())
+        pl.when(me + shift < n)(lambda shift=shift: hop(shift).wait_send())
+
+
+def gather_earlier(pair, n):
+    return pl.pallas_call(
+        lambda *refs: gather_kernel(n, *refs),
+        out_shape=jax.ShapeDtypeStruct((n * pair.shape[0], pair.shape[1]), pair.dtype),
+        in_specs=[pl.BlockSpec(memory_space=pltpu.VMEM)],
+        out_specs=pl.BlockSpec(memory_space=pltpu.VMEM),
+        scratch_shapes=[pltpu.SemaphoreType.DMA((n,)), pltpu.SemaphoreType.DMA((n,))],
+        compiler_params=pltpu.CompilerParams(collective_id=1, has_side_effects=True),
+    )(pair)
+
+
 def per_device(
     query_rows,
     key_rows,
@@ -265,11 +306,7 @@
     pair = jnp.concatenate([own_head(key_rows), own_head(value_rows)], axis=1)
     direct = ctx_count <= 4 and E % ctx_count == 0
     if direct:
-        pieces_kv = [pair]
-        for shift in range(1, ctx_count):
-            later = [(j, j + shift) for j in range(ctx_count - shift)]
-            pieces_kv.append(lax.ppermute(pair, "ctx", later))
-        pair = jnp.concatenate(pieces_kv, axis=0)
+        pair = gather_earlier(pair, ctx_count)
         column = jnp.arange(pair.shape[0], dtype=jnp.int32)
         key_pos = first_row + column - 2 * (column // row_count) * row_count
         visible = (query_pos[:, None] >= key_pos[None, :]) & (key_pos >= 0)[None, :]

time: 107 us -> 109 us (1.019)
  Pallas kernels: 82.8 us -> 96 us
  starting transfers between devices: 12.2 us -> 1.59 us
  waiting for transfers between devices: 3.19 us -> 2.05 us
    pallas_call x0 -> x1, Pallas kernels: none -> 10.8 us  [gather_earlier(): pl.pallas_call(lambda *refs: gather_kernel(n, *refs), out_shape=jax.Shape...]
    ppermute x3 -> x0, starting transfers between devices: 10.7 us -> none  [per_device(): pieces_kv.append(lax.ppermute(pair, 'ctx', later))]
    pallas_call x1, Pallas kernels: 82.8 us -> 85.2 us  [run_experts(): pl.pallas_call(lambda *refs: expert_kernel(n, held, pieces, *refs), out_s...]
    ppermute x2, waiting for transfers between devices: 3.17 us -> 2.05 us  [per_device(): lax.ppermute(stats, ('exp', 'tp'), [(j, j ^ flip) for j in range(ways)])]
    unnamed x10 -> x12, local copies, waits for them, and re-layouts: 2.22 us -> 1.55 us
  transfers between devices with their start and end apart: 5 -> 2, of which waited for: 2 -> 1; matrix products, arithmetic and copies ran while one was open for 3% -> 2% of each run, Pallas kernels for 0% -> 0%
where the time goes in v5:
time: 109 us
  Pallas kernels  96 us (88%)
  matrix products  3.71 us (3%)
  local copies, waits for them, and re-layouts  3.19 us (3%)
  other arithmetic  2.31 us (2%)
  waiting for transfers between devices  2.05 us (2%)
  starting transfers between devices  1.59 us (1%)
    pallas_call x1, Pallas kernels, run_experts(): pl.pallas_call(lambda *refs: expert_kernel(n, held, pieces, *refs), out_s...  85.2 us
    pallas_call x1, Pallas kernels, gather_earlier(): pl.pallas_call(lambda *refs: gather_kernel(n, *refs), out_shape=jax.Shape...  10.8 us
  transfers between devices with their start and end apart: 2, of which 1 were waited for; matrix products, arithmetic and copies ran while one was open for 2% of the time, Pallas kernels for 0%

profile of v5, /device:TPU:0, one launch (start us, length us, event | category | flops | bytes accessed | tf_op | source)
XLA Modules:
  0.0 109.1 jit_solution(11927737674436080757)
XLA Ops:
  0.0 0.0 copy-start
  0.0 0.8 constant_dynamic-slice_fusion
  0.8 0.6 pad_maximum_fusion.refs_0_
  1.5 10.8 %shard_map.91 = bf16[512,256]{1,0:T(8,128)(2,1)} custom-call(bf16[128,256]{1,0:T(8,128)(2,1)} %pad_maximum_fusion.refs_0_), custom_call_target="tpu_custom_call" | custom-call | tf_op jit(solution)/shard_map/pallas_call | solution.py:268
  12.3 1.1 copy.65
  13.4 0.2 compare_and_fusion
  13.6 0.0 copy-start.2
  13.6 1.3 %fusion.33 = (f32[6,128]{1,0:T(8,128)S(1)}, f32[6,128,512]{1,2,0:T(8,128)S(1)}) fusion(bf16[128,6,128]{0,2,1:T(8,128)(2,1)S(1)} %bitcast.47, bf16[512,256]{1,0:T(8,128)(2,1)} %shard_map.91, pred[128,512]{0,1:T(8,128)(4,1)S(1)} %compare_and_fusion), kind=kOutput, calls=%fused_computation.77 | convolution fusion | flops 101842176 | bytes 1969152 | tf_op jit(solution)/shard_map/tqd,sd->qts/dot_general | solution.py:317
  15.0 0.2 fusion
  15.2 0.0 copy-done.2
  15.2 0.0 copy-start.1
  15.2 0.0 copy-start.3
  15.2 0.4 fusion.2
  15.6 0.0 copy-start.4
  15.6 0.2 copy.69
  15.8 0.3 copy-done.1
  16.1 0.1 multiply_reduce_fusion
  16.3 0.0 copy-done
  16.3 0.0 copy-done.3
  16.3 0.4 fusion.7
  16.7 0.0 collective-permute-start
  16.8 0.0 copy-done.4
  16.8 0.1 copy.70
  16.9 0.1 eq.66
  17.0 0.1 eq.62
  17.2 0.6 reduce-window.6
  17.8 0.2 slice_reduce_fusion
  18.0 0.1 fusion.17
  18.1 0.1 reduce_sum.49
  18.3 0.1 copy.72
  18.4 0.0 collective-permute-done
  18.4 1.6 %collective-permute-start.1 = (f32[9,128]{1,0:T(8,128)S(1)}, f32[9,128]{1,0:T(8,128)S(1)}, u32[]{:S(2)}, u32[]{:S(2)}) collective-permute-start(f32[9,128]{1,0:T(8,128)S(1)} %fusion.32), channel_id=1, source_target_pairs={{0,2},{1,3},{2,0},{3,1},{4,6},{5,7},{6,4},{7,5},{8,10},{9,11},{10,... | collective-permute-start | bytes 13832 | tf_op jit(solution)/shard_map/ppermute | solution.py:338
  20.0 0.1 fusion.6
  20.1 2.1 %collective-permute-done.1 = f32[9,128]{1,0:T(8,128)S(1)} collective-permute-done((f32[9,128]{1,0:T(8,128)S(1)}, f32[9,128]{1,0:T(8,128)S(1)}, u32[]{:S(2)}, u32[]{:S(2)}) %collective-permute-start.1) | collective-permute-done | bytes 4640 | tf_op jit(solution)/shard_map/ppermute | solution.py:338
  22.1 0.4 convolution_convert_fusion
  22.6 0.1 select_reduce_fusion
  22.7 85.2 %shard_map.92 = bf16[4,96,768]{2,1,0:T(8,128)(2,1)S(1)} custom-call(bf16[4,96,768]{2,1,0:T(8,128)(2,1)S(1)} %bitcast.44, bf16[1536,8192]{1,0:T(8,128)(2,1)} %bitcast.45, bf16[8192,1536]{1,0:T(8,128)(2,1)} %bitcast.46), custom_call_target="tpu_custom_call" | custom-call | flops 9663676416 | bytes 100663296 | tf_op jit(solution)/shard_map/pallas_call | solution.py:200
  107.9 1.1 %fusion.3 = bf16[128,768]{1,0:T(8,128)(2,1)} fusion(f32[128,384]{1,0:T(8,128)S(1)} %select_reduce_fusion, bf16[384,768]{1,0:T(8,128)(2,1)S(1)} %bitcast.43, f32[128,768]{1,0:T(8,128)S(1)} %copy.69, bf16[128,768]{1,0:T(8,128)(2,1)S(1)} %copy-done.1), kind=kOutput, calls=%fused_computation.8 | convolution fusion | flops 453378048 | bytes 1572864 | tf_op jit(solution)/shard_map/dot_general | solution.py:389
  (15 shorter events, 0.2 us)
Async XLA Ops:
  0.0 16.3 %copy-start = (f32[768,8]{0,1:T(8,128)S(1)}, f32[768,8]{0,1:T(8,128)}, u32[]{:S(2)}) copy-start(f32[768,8]{0,1:T(8,128)} %param.14) | copy-start | bytes 73732
  13.6 1.6 %copy-start.2 = (bf16[512,256]{1,0:T(8,128)(2,1)S(1)}, bf16[512,256]{1,0:T(8,128)(2,1)}, u32[]{:S(2)}) copy-start(bf16[512,256]{1,0:T(8,128)(2,1)} %shard_map.91) | copy-start | bytes 786436
  15.2 0.9 copy-start.1
  15.2 1.1 copy-start.3
  15.6 1.1 %copy-start.4 = (s32[128,2]{0,1:T(2,128)S(1)}, s32[128,2]{0,1:T(2,128)}, u32[]{:S(2)}) copy-start(s32[128,2]{0,1:T(2,128)} %param.15) | copy-start | bytes 3076
  16.7 1.7 %collective-permute-start = (f32[9,128]{1,0:T(8,128)S(1)}, f32[9,128]{1,0:T(8,128)S(1)}, u32[]{:S(2)}, u32[]{:S(2)}) collective-permute-start(f32[9,128]{1,0:T(8,128)S(1)} %maximum_bitcast_fusion), channel_id=1, source_target_pairs={{0,1},{1,0},{2,3},{3,2},{4,5},{5,4},{6,7},{7,6},{8,9},{9,8},{10,11... | collective-permute-start | bytes 13832 | tf_op jit(solution)/shard_map/ppermute | solution.py:338
  18.4 3.7 %collective-permute-start.1 = (f32[9,128]{1,0:T(8,128)S(1)}, f32[9,128]{1,0:T(8,128)S(1)}, u32[]{:S(2)}, u32[]{:S(2)}) collective-permute-start(f32[9,128]{1,0:T(8,128)S(1)} %fusion.32), channel_id=1, source_target_pairs={{0,2},{1,3},{2,0},{3,1},{4,6},{5,7},{6,4},{7,5},{8,10},{9,11},{10,... | collective-permute-start | bytes 13832 | tf_op jit(solution)/shard_map/ppermute | solution.py:338

commit v6 on v4

--- a/solution.py
+++ b/solution.py
@@ -297,8 +297,11 @@
     ways = exp_count * tp_count
     if ways == 4:
         stats = jnp.concatenate([logit_part, square_sum[:, None]], axis=1).T
-        for flip in (1, 2):
-            stats = stats + lax.ppermute(stats, ("exp", "tp"), [(j, j ^ flip) for j in range(ways)])
+        others = [
+            lax.ppermute(stats, ("exp", "tp"), [(j, j ^ flip) for j in range(ways)])
+            for flip in (1, 2, 3)
+        ]
+        stats = (stats + others[0]) + (others[1] + others[2])
         logit_part, square_sum = stats[:E].T, stats[E]
     else:
         square_sum, logit_part = lax.psum((square_sum, logit_part), ("exp", "tp"))

time: 107 us -> 106 us (level)
  Pallas kernels: 82.8 us -> 81.2 us
    pallas_call x1, Pallas kernels: 82.8 us -> 81.2 us  [run_experts(): pl.pallas_call(lambda *refs: expert_kernel(n, held, pieces, *refs), out_s...]
    ppermute x2 -> x3, waiting for transfers between devices: 3.17 us -> 2.65 us  [per_device(): lax.ppermute(stats, ('exp', 'tp'), [(j, j ^ flip) for j in range(ways)])]
  transfers between devices with their start and end apart: 5 -> 6, of which waited for: 2 -> 2; matrix products, arithmetic and copies ran while one was open for 3% -> 4% of each run, Pallas kernels for 0% -> 0%
where the time goes in v6:
time: 106 us
  Pallas kernels  81.2 us (77%)
  starting transfers between devices  12.6 us (12%)
  local copies, waits for them, and re-layouts  3.86 us (4%)
  matrix products  2.74 us (3%)
  waiting for transfers between devices  2.66 us (3%)
  other arithmetic  2.38 us (2%)
    pallas_call x1, Pallas kernels, run_experts(): pl.pallas_call(lambda *refs: expert_kernel(n, held, pieces, *refs), out_s...  81.2 us
    ppermute x3, starting transfers between devices, per_device(): pieces_kv.append(lax.ppermute(pair, 'ctx', later))  10.7 us
    ppermute x3, waiting for transfers between devices, per_device(): lax.ppermute(stats, ('exp', 'tp'), [(j, j ^ flip) for j in range(ways)])  2.65 us
    unnamed x10, local copies, waits for them, and re-layouts  2.21 us
  transfers between devices with their start and end apart: 6, of which 2 were waited for; matrix products, arithmetic and copies ran while one was open for 4% of the time, Pallas kernels for 0%

profile of v6, /device:TPU:0, one launch (start us, length us, event | category | flops | bytes accessed | tf_op | source)
XLA Modules:
  0.0 105.7 jit_solution(15483263430254631679)
XLA Ops:
  0.0 0.0 copy-start
  0.0 0.8 constant_dynamic-slice_fusion
  0.8 4.9 %collective-permute-start = (bf16[128,256]{1,0:T(8,128)(2,1)S(1)}, bf16[128,256]{1,0:T(8,128)(2,1)S(1)}, u32[]{:S(2)}, u32[]{:S(2)}) collective-permute-start(bf16[128,256]{1,0:T(8,128)(2,1)S(1)} %pad_maximum_fusion.1), channel_id=1, source_target_pairs={{0,4},{4,8},{8,12},{1,5},{5,9},{9,13},{2,6},{6,10},{10,14},{3,7},{... | collective-permute-start | bytes 196616 | tf_op jit(solution)/shard_map/ppermute | solution.py:271
  5.7 4.5 %collective-permute-start.1 = (bf16[128,256]{1,0:T(8,128)(2,1)S(1)}, bf16[128,256]{1,0:T(8,128)(2,1)S(1)}, u32[]{:S(2)}, u32[]{:S(2)}) collective-permute-start(bf16[128,256]{1,0:T(8,128)(2,1)S(1)} %pad_maximum_fusion.1), channel_id=1, source_target_pairs={{0,8},{4,12},{1,9},{5,13},{2,10},{6,14},{3,11},{7,15},{16,24},{20,... | collective-permute-start | bytes 196616 | tf_op jit(solution)/shard_map/ppermute | solution.py:271
  10.2 1.3 %collective-permute-start.2 = (bf16[128,256]{1,0:T(8,128)(2,1)S(1)}, bf16[128,256]{1,0:T(8,128)(2,1)S(1)}, u32[]{:S(2)}, u32[]{:S(2)}) collective-permute-start(bf16[128,256]{1,0:T(8,128)(2,1)S(1)} %pad_maximum_fusion.1), channel_id=1, source_target_pairs={{0,12},{1,13},{2,14},{3,15},{16,28},{17,29},{18,30},{19,31}} | collective-permute-start | bytes 196616 | tf_op jit(solution)/shard_map/ppermute | solution.py:271
  11.6 0.8 copy.70
  12.4 0.1 eq.66
  12.5 0.1 eq.62
  12.7 0.6 reduce-window.6
  13.3 0.2 slice_reduce_fusion
  13.5 0.1 fusion.13
  13.6 0.1 reduce_sum.49
  13.8 0.1 copy.72
  13.8 0.2 compare_and_fusion
  14.0 0.7 multiply_add_fusion
  14.8 1.1 %copy.65 = bf16[128,768]{0,1:T(8,128)(2,1)S(1)} copy(bf16[128,768]{1,0:T(8,128)(2,1)} %param.9) | data formatting | bytes 393216 | tf_op args[0]
  15.8 0.0 collective-permute-done
  15.9 0.0 collective-permute-done.1
  15.9 0.0 collective-permute-done.2
  15.9 0.4 fusion.28
  16.3 0.2 fusion
  16.5 0.0 copy-start.1
  16.5 0.0 copy-start.2
  16.6 0.4 fusion.2
  17.0 0.0 copy-start.3
  17.0 0.2 copy.69
  17.1 0.3 copy-done.1
  17.5 0.1 multiply_reduce_fusion
  17.6 0.0 copy-done
  17.6 0.0 copy-done.2
  17.6 0.4 fusion.7
  18.0 0.0 collective-permute-start.3
  18.1 1.6 %collective-permute-start.4 = (f32[9,128]{1,0:T(8,128)S(1)}, f32[9,128]{1,0:T(8,128)S(1)}, u32[]{:S(2)}, u32[]{:S(2)}) collective-permute-start(f32[9,128]{1,0:T(8,128)S(1)} %maximum_bitcast_fusion), channel_id=1, source_target_pairs={{0,2},{1,3},{2,0},{3,1},{4,6},{5,7},{6,4},{7,5},{8,10},{9,11},{10,... | collective-permute-start | bytes 13832 | tf_op jit(solution)/shard_map/ppermute | solution.py:301
  19.6 0.3 collective-permute-start.5
  19.9 0.1 fusion.6
  20.0 0.0 collective-permute-done.3
  20.1 1.7 %collective-permute-done.4 = f32[9,128]{1,0:T(8,128)S(1)} collective-permute-done((f32[9,128]{1,0:T(8,128)S(1)}, f32[9,128]{1,0:T(8,128)S(1)}, u32[]{:S(2)}, u32[]{:S(2)}) %collective-permute-start.4) | collective-permute-done | bytes 4640 | tf_op jit(solution)/shard_map/ppermute | solution.py:301
  21.8 0.9 collective-permute-done.5
  22.7 0.4 convolution_convert_fusion
  23.1 0.0 copy-done.3
  23.2 0.1 select_reduce_fusion
  23.4 81.2 %shard_map.91 = bf16[4,96,768]{2,1,0:T(8,128)(2,1)S(1)} custom-call(bf16[4,96,768]{2,1,0:T(8,128)(2,1)S(1)} %bitcast.44, bf16[1536,8192]{1,0:T(8,128)(2,1)} %bitcast.45, bf16[8192,1536]{1,0:T(8,128)(2,1)} %bitcast.46), custom_call_target="tpu_custom_call" | custom-call | flops 9663676416 | bytes 100663296 | tf_op jit(solution)/shard_map/pallas_call | solution.py:200
  104.6 1.1 %fusion.3 = bf16[128,768]{1,0:T(8,128)(2,1)} fusion(f32[128,384]{1,0:T(8,128)S(1)} %select_reduce_fusion, bf16[384,768]{1,0:T(8,128)(2,1)S(1)} %bitcast.43, f32[128,768]{1,0:T(8,128)S(1)} %copy.69, bf16[128,768]{1,0:T(8,128)(2,1)S(1)} %copy-done.1), kind=kOutput, calls=%fused_computation.8 | convolution fusion | flops 453378048 | bytes 1572864 | tf_op jit(solution)/shard_map/dot_general | solution.py:355
  (15 shorter events, 0.2 us)
Async XLA Ops:
  0.0 17.6 %copy-start = (f32[768,8]{0,1:T(8,128)S(1)}, f32[768,8]{0,1:T(8,128)}, u32[]{:S(2)}) copy-start(f32[768,8]{0,1:T(8,128)} %param.14) | copy-start | bytes 73732
  0.8 15.0 %collective-permute-start = (bf16[128,256]{1,0:T(8,128)(2,1)S(1)}, bf16[128,256]{1,0:T(8,128)(2,1)S(1)}, u32[]{:S(2)}, u32[]{:S(2)}) collective-permute-start(bf16[128,256]{1,0:T(8,128)(2,1)S(1)} %pad_maximum_fusion.1), channel_id=1, source_target_pairs={{0,4},{4,8},{8,12},{1,5},{5,9},{9,13},{2,6},{6,10},{10,14},{3,7},{... | collective-permute-start | bytes 196616 | tf_op jit(solution)/shard_map/ppermute | solution.py:271
  5.7 10.1 %collective-permute-start.1 = (bf16[128,256]{1,0:T(8,128)(2,1)S(1)}, bf16[128,256]{1,0:T(8,128)(2,1)S(1)}, u32[]{:S(2)}, u32[]{:S(2)}) collective-permute-start(bf16[128,256]{1,0:T(8,128)(2,1)S(1)} %pad_maximum_fusion.1), channel_id=1, source_target_pairs={{0,8},{4,12},{1,9},{5,13},{2,10},{6,14},{3,11},{7,15},{16,24},{20,... | collective-permute-start | bytes 196616 | tf_op jit(solution)/shard_map/ppermute | solution.py:271
  10.2 5.6 %collective-permute-start.2 = (bf16[128,256]{1,0:T(8,128)(2,1)S(1)}, bf16[128,256]{1,0:T(8,128)(2,1)S(1)}, u32[]{:S(2)}, u32[]{:S(2)}) collective-permute-start(bf16[128,256]{1,0:T(8,128)(2,1)S(1)} %pad_maximum_fusion.1), channel_id=1, source_target_pairs={{0,12},{1,13},{2,14},{3,15},{16,28},{17,29},{18,30},{19,31}} | collective-permute-start | bytes 196616 | tf_op jit(solution)/shard_map/ppermute | solution.py:271
  16.5 0.9 copy-start.1
  16.5 1.1 copy-start.2
  17.0 6.2 %copy-start.3 = (s32[128,2]{0,1:T(2,128)S(1)}, s32[128,2]{0,1:T(2,128)}, u32[]{:S(2)}) copy-start(s32[128,2]{0,1:T(2,128)} %param.15) | copy-start | bytes 3076
  18.0 2.0 %collective-permute-start.3 = (f32[9,128]{1,0:T(8,128)S(1)}, f32[9,128]{1,0:T(8,128)S(1)}, u32[]{:S(2)}, u32[]{:S(2)}) collective-permute-start(f32[9,128]{1,0:T(8,128)S(1)} %maximum_bitcast_fusion), channel_id=1, source_target_pairs={{0,1},{1,0},{2,3},{3,2},{4,5},{5,4},{6,7},{7,6},{8,9},{9,8},{10,11... | collective-permute-start | bytes 13832 | tf_op jit(solution)/shard_map/ppermute | solution.py:301
  18.1 3.7 %collective-permute-start.4 = (f32[9,128]{1,0:T(8,128)S(1)}, f32[9,128]{1,0:T(8,128)S(1)}, u32[]{:S(2)}, u32[]{:S(2)}) collective-permute-start(f32[9,128]{1,0:T(8,128)S(1)} %maximum_bitcast_fusion), channel_id=1, source_target_pairs={{0,2},{1,3},{2,0},{3,1},{4,6},{5,7},{6,4},{7,5},{8,10},{9,11},{10,... | collective-permute-start | bytes 13832 | tf_op jit(solution)/shard_map/ppermute | solution.py:301
  19.6 3.1 %collective-permute-start.5 = (f32[9,128]{1,0:T(8,128)S(1)}, f32[9,128]{1,0:T(8,128)S(1)}, u32[]{:S(2)}, u32[]{:S(2)}) collective-permute-start(f32[9,128]{1,0:T(8,128)S(1)} %maximum_bitcast_fusion), channel_id=1, source_target_pairs={{0,3},{1,2},{2,1},{3,0},{4,7},{5,6},{6,5},{7,4},{8,11},{9,10},{10,... | collective-permute-start | bytes 13832 | tf_op jit(solution)/shard_map/ppermute | solution.py:301
